TPU v7x, 32 devices: a whole 2x2x4 slice. The times are simulated.
32 devices in a mesh: dp: 16 (over z, x, core), mp: 2 (over y).
Axes of the slice: x: 2, y: 2, z: 4, core: 2. Of those that a mesh axis runs over, the one named last changes fastest.
Arguments:
- hidden_in: bfloat16 [16, 1024, 768], P('dp'), may hold values from -6 to 6, as said below
- segment_ids: int32 [16, 1024], P('dp'), may hold values from 0 to 7, as said below
- time_mask: int32 [16, 1024], P('dp'), may hold values 0 or 1
- mask_embed: bfloat16 [768], replicated, may hold values from -4 to 4
- conv_weight: bfloat16 [6144, 768], P('dp', 'mp'), may hold values from -0.078125 to 0.078125
- conv_bias: bfloat16 [768], P('mp'), may hold values from -3 to 3
- query_weight: bfloat16 [768, 768], P('dp', 'mp'), may hold values from -0.21875 to 0.21875
- key_weight: bfloat16 [768, 768], P('dp', 'mp'), may hold values from -0.21875 to 0.21875
- value_weight: bfloat16 [768, 768], P('dp', 'mp'), may hold values from -0.21875 to 0.21875
- query_bias: bfloat16 [768], P('mp'), may hold values from -3 to 3
- value_bias: bfloat16 [768], P('mp'), may hold values from -3 to 3
- out_weight: bfloat16 [768, 768], P('mp', 'dp'), may hold values from -1.75 to 1.75
- out_bias: bfloat16 [768], replicated, may hold values from -3 to 3
- first_gain: bfloat16 [768], replicated, may hold values from 0.099609375 to 1.8984375
- first_shift: bfloat16 [768], replicated, may hold values from -3 to 3
- up_weight: bfloat16 [768, 3072], P('dp', 'mp'), may hold values from -0.21875 to 0.21875
- up_bias: bfloat16 [3072], P('mp'), may hold values from -3 to 3
- down_weight: bfloat16 [3072, 768], P('mp', 'dp'), may hold values from -0.109375 to 0.109375
- down_bias: bfloat16 [768], replicated, may hold values from -3 to 3
- second_gain: bfloat16 [768], replicated, may hold values from 0.099609375 to 1.8984375
- second_shift: bfloat16 [768], replicated, may hold values from -3 to 3
- cotangent: bfloat16 [16, 1024, 768], P('dp'), may hold values from -6 to 6
Outputs:
- layer_out: bfloat16 [16, 1024, 768], P('dp')
- input_grad: float32 [16, 1024, 768], P('dp', None, 'mp')
- mask_grad: float32 [768], P('mp')
- conv_grad: float32 [6144, 768], P('dp', 'mp')
- conv_bias_grad: float32 [768], P('mp')
- query_grad: float32 [768, 768], P('dp', 'mp')
- key_grad: float32 [768, 768], P('dp', 'mp')
- value_grad: float32 [768, 768], P('dp', 'mp')
- query_bias_grad: float32 [768], P('mp')
- value_bias_grad: float32 [768], P('mp')
- out_grad: float32 [768, 768], P('mp', 'dp')
- out_bias_grad: float32 [768], replicated
- first_gain_grad: float32 [768], replicated
- first_shift_grad: float32 [768], replicated
- up_grad: float32 [768, 3072], P('dp', 'mp')
- up_bias_grad: float32 [3072], P('mp')
- down_grad: float32 [3072, 768], P('mp', 'dp')
- down_bias_grad: float32 [768], replicated
- second_gain_grad: float32 [768], replicated
- second_shift_grad: float32 [768], replicated
- stream_rms: float32 [4], replicated
Inputs may be any that keep to these rules, and one draw needn't show every extreme that they name: `hidden_in`: scaled by a factor per packed row; rows later in the array are larger. `segment_ids`: along a row the ids never fall until the padding (id 0), which fills the end of the row; a row starts with id 1 and holds fewer than 512 padding frames.
All inputs are finite; a program needn't handle non-finite values. No bound on the sum of `time_mask` on one device may be relied on, other than what follows from the above.
Results may differ from a plain program's by a relative error of at most 0.02.
Values may be sent and summed in bfloat16 or wider, within the bound.
A program may use at most 192 MiB of HBM per device.

v0:
```python
import jax
import jax.numpy as jnp
from jax import lax
from jax.sharding import PartitionSpec as P

HD = 64
KW = 128
CG = 48


tap_block = 16
norm_eps = 1e-05


def exact_gelu(values):
    return jax.nn.gelu(values, approximate=False)


def layer_norm(rows, gain, shift):
    centre = rows - jnp.mean(rows, axis=-1, keepdims=True)
    spread = jnp.mean(centre * centre, axis=-1, keepdims=True)
    return centre * lax.rsqrt(spread + norm_eps) * gain + shift


def matmul(left, right):
    return jnp.dot(left, right, preferred_element_type=jnp.float32)


def masked_taps(padded, seg_pad, seg_here, offsets):
    length = seg_here.shape[1]
    pieces = []
    for offset in offsets:
        window = lax.dynamic_slice_in_dim(padded, offset, length, 3)
        neighbour = lax.dynamic_slice_in_dim(seg_pad, offset, length, 1)
        keep_mask = (neighbour == seg_here)[:, None, None, :]
        pieces.append(jnp.where(keep_mask, window, jnp.zeros_like(window)))
    stacked = jnp.stack(pieces, axis=2)
    padded_dims = padded.shape
    return stacked.reshape(padded_dims[0], padded_dims[1], len(offsets) * padded_dims[2], length)


def attend_block(query_blk, keys_row, values_row, seg_blk, seg_row, scale):
    scores = (
        jnp.einsum("qhd,khd->hqk", query_blk, keys_row, preferred_element_type=jnp.float32) * scale
    )
    allowed = (seg_blk[:, None] == seg_row[None, :])[None]
    scores = jnp.where(allowed, scores, -1000000000.0)
    top_score = jnp.max(scores, axis=-1, keepdims=True)
    expo = jnp.exp(scores - top_score)
    denom = jnp.sum(expo, axis=-1, keepdims=True)
    weights = (expo / denom).astype(jnp.bfloat16)
    context = jnp.einsum("hqk,khd->qhd", weights, values_row, preferred_element_type=jnp.float32)
    return (context, (top_score + jnp.log(denom))[..., 0])


def attention_rows(queries, keys_all, values_all, segment_ids, qblock, scale):

    def one_row(row_items):
        query_row, keys_row, values_row, seg_row = row_items
        block_query = query_row.reshape(-1, qblock, query_row.shape[1], query_row.shape[2])
        block_seg = seg_row.reshape(-1, qblock)

        def one_block(block_items):
            return attend_block(
                block_items[0], keys_row, values_row, block_items[1], seg_row, scale
            )

        return lax.map(one_block, (block_query, block_seg))

    return lax.map(one_row, (queries, keys_all, values_all, segment_ids))


def attention_back_rows(
    queries, keys_all, values_all, segment_ids, lse_all, grad_context, qblock, scale
):

    def one_row(row_items):
        query_row, keys_row, values_row, seg_row, lse_row, grad_row = row_items
        heads_here = query_row.shape[1]
        head_size = query_row.shape[2]
        blocks = (
            query_row.reshape(-1, qblock, heads_here, head_size),
            seg_row.reshape(-1, qblock),
            lse_row,
            grad_row.reshape(-1, qblock, heads_here, head_size),
        )

        def one_block(carry, block_items):
            key_grad, value_grad = carry
            query_blk, seg_blk, lse_blk, dout_blk = block_items
            scores = (
                jnp.einsum("qhd,khd->hqk", query_blk, keys_row, preferred_element_type=jnp.float32)
                * scale
            )
            allowed = (seg_blk[:, None] == seg_row[None, :])[None]
            scores = jnp.where(allowed, scores, -1000000000.0)
            probs = jnp.exp(scores - lse_blk[..., None])
            probs_low = probs.astype(jnp.bfloat16)
            value_grad = value_grad + jnp.einsum(
                "hqk,qhd->khd", probs_low, dout_blk, preferred_element_type=jnp.float32
            )
            prob_grad = jnp.einsum(
                "qhd,khd->hqk", dout_blk, values_row, preferred_element_type=jnp.float32
            )
            inner_sum = jnp.sum(probs * prob_grad, axis=-1, keepdims=True)
            score_grad = (probs * (prob_grad - inner_sum)).astype(jnp.bfloat16)
            query_grad = (
                jnp.einsum("hqk,khd->qhd", score_grad, keys_row, preferred_element_type=jnp.float32)
                * scale
            )
            key_grad = (
                key_grad
                + jnp.einsum(
                    "hqk,qhd->khd", score_grad, query_blk, preferred_element_type=jnp.float32
                )
                * scale
            )
            return ((key_grad, value_grad), query_grad.astype(jnp.bfloat16))

        zeros_kv = jnp.zeros(keys_row.shape, jnp.float32)
        (key_grad, value_grad), query_grad = lax.scan(one_block, (zeros_kv, zeros_kv), blocks)
        return (query_grad, key_grad.astype(jnp.bfloat16), value_grad.astype(jnp.bfloat16))

    return lax.map(one_row, (queries, keys_all, values_all, segment_ids, lse_all, grad_context))


def local(
    hidden_in,
    segment_ids,
    time_mask,
    mask_embed,
    conv_weight,
    conv_bias,
    query_weight,
    key_weight,
    value_weight,
    query_bias,
    value_bias,
    out_weight,
    out_bias,
    first_gain,
    first_shift,
    up_weight,
    up_bias,
    down_weight,
    down_bias,
    second_gain,
    second_shift,
    cotangent,
):
    rows_here, length, width = hidden_in.shape
    local_width = query_weight.shape[1]
    local_groups = local_width // CG
    heads_here = local_width // HD
    qblock = min(512, length)
    scale = HD ** (-0.5)
    tokens = rows_here * length
    my_part = lax.axis_index("mp")
    gathered = (
        lax.all_gather(conv_weight, "dp", axis=0, tiled=True),
        lax.all_gather(query_weight, "dp", axis=0, tiled=True),
        lax.all_gather(key_weight, "dp", axis=0, tiled=True),
        lax.all_gather(value_weight, "dp", axis=0, tiled=True),
        lax.all_gather(out_weight, "dp", axis=1, tiled=True),
        lax.all_gather(up_weight, "dp", axis=0, tiled=True),
        lax.all_gather(down_weight, "dp", axis=1, tiled=True),
    )
    conv_full, query_full, key_full, value_full, out_full, up_full, down_full = gathered
    valid_rows = (segment_ids != 0).astype(jnp.float32)
    masked = time_mask.astype(jnp.float32)
    inputs = hidden_in.astype(jnp.float32)
    start_in = inputs + masked[..., None] * (mask_embed.astype(jnp.float32) - inputs)
    start_low = start_in.astype(jnp.bfloat16)
    local_in = lax.dynamic_slice_in_dim(start_low, my_part * local_width, local_width, 2)
    chan_first = local_in.transpose(0, 2, 1).reshape(rows_here, local_groups, CG, length)
    half_kernel = KW // 2
    padded_in = jnp.pad(chan_first, ((0, 0), (0, 0), (0, 0), (half_kernel, half_kernel)))
    seg_pad = jnp.pad(segment_ids, ((0, 0), (half_kernel, half_kernel)), constant_values=-1)
    kernel = conv_full.reshape(KW, CG, local_groups, CG)
    forward_taps = kernel.transpose(2, 3, 0, 1).reshape(local_groups, CG, KW * CG)
    block_ids = jnp.arange(KW // tap_block, dtype=jnp.int32)

    def conv_step(total, block_id):
        first_tap = block_id * tap_block
        patches = masked_taps(
            padded_in,
            seg_pad,
            segment_ids,
            [first_tap + offset_in for offset_in in range(tap_block)],
        )
        taps_now = lax.dynamic_slice_in_dim(forward_taps, first_tap * CG, tap_block * CG, 2)
        return (
            total
            + jnp.einsum("gom,rgmt->rgot", taps_now, patches, preferred_element_type=jnp.float32),
            None,
        )

    conv_sum, _ = lax.scan(
        conv_step, jnp.zeros((rows_here, local_groups, CG, length), jnp.float32), block_ids
    )
    conv_pre = conv_sum.reshape(rows_here, local_width, length).transpose(
        0, 2, 1
    ) + conv_bias.astype(jnp.float32)
    conv_low = (valid_rows[..., None] * exact_gelu(conv_pre)).astype(jnp.bfloat16)
    conv_all = lax.all_gather(conv_low, "mp", axis=2, tiled=True).astype(jnp.float32)
    mixed = (start_in + conv_all).reshape(tokens, width)
    mixed_low = mixed.astype(jnp.bfloat16)
    queries = (matmul(mixed_low, query_full) + query_bias.astype(jnp.float32)).astype(jnp.bfloat16)
    keys_all = matmul(mixed_low, key_full).astype(jnp.bfloat16)
    values_all = (matmul(mixed_low, value_full) + value_bias.astype(jnp.float32)).astype(
        jnp.bfloat16
    )
    head_shape = (rows_here, length, heads_here, HD)
    queries4 = queries.reshape(head_shape)
    keys4 = keys_all.reshape(head_shape)
    values4 = values_all.reshape(head_shape)
    context, lse_all = attention_rows(queries4, keys4, values4, segment_ids, qblock, scale)
    valid_flat = valid_rows.reshape(tokens, 1)
    ctx_low = (context.reshape(tokens, local_width) * valid_flat).astype(jnp.bfloat16)
    attn_out = lax.psum(matmul(ctx_low, out_full).astype(jnp.bfloat16), "mp").astype(
        jnp.float32
    ) + out_bias.astype(jnp.float32)
    resid_one = mixed + attn_out
    gain_one = first_gain.astype(jnp.float32)
    shift_one = first_shift.astype(jnp.float32)
    normed_one = layer_norm(resid_one, gain_one, shift_one)
    normed_low = normed_one.astype(jnp.bfloat16)
    hidden_pre = matmul(normed_low, up_full) + up_bias.astype(jnp.float32)
    hidden_low = exact_gelu(hidden_pre).astype(jnp.bfloat16)
    ffn_out = lax.psum(matmul(hidden_low, down_full).astype(jnp.bfloat16), "mp").astype(
        jnp.float32
    ) + down_bias.astype(jnp.float32)
    resid_two = normed_one + ffn_out
    gain_two = second_gain.astype(jnp.float32)
    shift_two = second_shift.astype(jnp.float32)
    normed_two = layer_norm(resid_two, gain_two, shift_two)
    final = valid_flat * normed_two
    layer_out = final.astype(jnp.bfloat16).reshape(rows_here, length, width)
    conv_flat = conv_all.reshape(tokens, width)
    stats = jnp.stack(
        [
            jnp.sum(valid_flat * conv_flat * conv_flat),
            jnp.sum(valid_flat * attn_out * attn_out),
            jnp.sum(valid_flat * ffn_out * ffn_out),
            jnp.sum(final * final),
        ]
    )
    frame_count = jnp.sum(valid_rows)
    conv_back, query_back, key_back, value_back, out_back, up_back, down_back = gathered
    grad_final = cotangent.astype(jnp.float32).reshape(tokens, width) * valid_flat
    _, norm_two_back = jax.vjp(layer_norm, resid_two, gain_two, shift_two)
    grad_resid_two, grad_gain_two, grad_shift_two = norm_two_back(grad_final)
    ffn_grad = grad_resid_two.astype(jnp.bfloat16)
    grad_down_bias = jnp.sum(ffn_grad.astype(jnp.float32), axis=0)
    grad_down = jnp.einsum("nf,nd->fd", hidden_low, ffn_grad, preferred_element_type=jnp.float32)
    grad_hidden = jnp.einsum("nd,fd->nf", ffn_grad, down_back, preferred_element_type=jnp.float32)
    _, hidden_gelu_back = jax.vjp(exact_gelu, hidden_pre)
    hidden_grad = hidden_gelu_back(grad_hidden)[0].astype(jnp.bfloat16)
    grad_up_bias = jnp.sum(hidden_grad.astype(jnp.float32), axis=0)
    grad_up = jnp.einsum("nd,nf->df", normed_low, hidden_grad, preferred_element_type=jnp.float32)
    down_done, up_done = (grad_down, grad_up)
    from_ffn = lax.psum(
        jnp.einsum("nf,df->nd", hidden_grad, up_back, preferred_element_type=jnp.float32).astype(
            jnp.bfloat16
        ),
        "mp",
    ).astype(jnp.float32)
    grad_normed_one = grad_resid_two + from_ffn
    _, norm_one_back = jax.vjp(layer_norm, resid_one, gain_one, shift_one)
    grad_resid_one, grad_gain_one, grad_shift_one = norm_one_back(grad_normed_one)
    attn_grad = grad_resid_one.astype(jnp.bfloat16)
    grad_out_bias = jnp.sum(attn_grad.astype(jnp.float32), axis=0)
    grad_out = jnp.einsum("nc,nd->cd", ctx_low, attn_grad, preferred_element_type=jnp.float32)
    context_grad = jnp.einsum(
        "nd,cd->nc", attn_grad, out_back, preferred_element_type=jnp.float32
    ).astype(jnp.bfloat16)
    context_grad = jnp.where(valid_flat > 0, context_grad, jnp.zeros_like(context_grad))
    query_grad, key_grad, value_grad = attention_back_rows(
        queries4,
        keys4,
        values4,
        segment_ids,
        lse_all,
        context_grad.reshape(head_shape),
        qblock,
        scale,
    )
    query_grad = query_grad.reshape(tokens, local_width)
    key_grad = key_grad.reshape(tokens, local_width)
    value_grad = value_grad.reshape(tokens, local_width)
    grad_query = jnp.einsum("nd,nc->dc", mixed_low, query_grad, preferred_element_type=jnp.float32)
    grad_key = jnp.einsum("nd,nc->dc", mixed_low, key_grad, preferred_element_type=jnp.float32)
    grad_value = jnp.einsum("nd,nc->dc", mixed_low, value_grad, preferred_element_type=jnp.float32)
    grad_query_bias = jnp.sum(query_grad.astype(jnp.float32), axis=0)
    grad_value_bias = jnp.sum(value_grad.astype(jnp.float32), axis=0)
    query_done, key_done, value_done, out_done = (grad_query, grad_key, grad_value, grad_out)
    qkv_terms = (
        jnp.einsum("nc,dc->nd", query_grad, query_back, preferred_element_type=jnp.float32)
        + jnp.einsum("nc,dc->nd", key_grad, key_back, preferred_element_type=jnp.float32)
        + jnp.einsum("nc,dc->nd", value_grad, value_back, preferred_element_type=jnp.float32)
    )
    from_qkv = lax.psum(qkv_terms.astype(jnp.bfloat16), "mp").astype(jnp.float32)
    grad_mixed = (grad_resid_one + from_qkv).reshape(rows_here, length, width)
    grad_local = lax.dynamic_slice_in_dim(grad_mixed, my_part * local_width, local_width, 2)
    _, conv_gelu_back = jax.vjp(exact_gelu, conv_pre)
    conv_pre_grad = conv_gelu_back(grad_local * valid_rows[..., None])[0].astype(jnp.bfloat16)
    grad_conv_bias = jnp.sum(conv_pre_grad.astype(jnp.float32), axis=(0, 1))
    grad_chan = conv_pre_grad.transpose(0, 2, 1).reshape(rows_here, local_groups, CG, length)
    padded_grad = jnp.pad(grad_chan, ((0, 0), (0, 0), (0, 0), (half_kernel, half_kernel)))
    kernel_back = conv_back.reshape(KW, CG, local_groups, CG)
    back_taps = kernel_back.transpose(2, 1, 0, 3).reshape(local_groups, CG, KW * CG)

    def conv_back_step(total, block_id):
        first_tap = block_id * tap_block
        patches = masked_taps(
            padded_in,
            seg_pad,
            segment_ids,
            [first_tap + offset_in for offset_in in range(tap_block)],
        )
        weight_piece = jnp.einsum(
            "rgmt,rgot->gmo", patches, grad_chan, preferred_element_type=jnp.float32
        )
        spread_grad = masked_taps(
            padded_grad,
            seg_pad,
            segment_ids,
            [KW - first_tap - offset_in for offset_in in range(tap_block)],
        )
        taps_now = lax.dynamic_slice_in_dim(back_taps, first_tap * CG, tap_block * CG, 2)
        total = total + jnp.einsum(
            "gim,rgmt->rgit", taps_now, spread_grad, preferred_element_type=jnp.float32
        )
        return (total, weight_piece)

    input_back, weight_pieces = lax.scan(
        conv_back_step, jnp.zeros((rows_here, local_groups, CG, length), jnp.float32), block_ids
    )
    grad_conv = weight_pieces.reshape(KW // tap_block, local_groups, tap_block, CG, CG).transpose(
        0, 2, 3, 1, 4
    )
    grad_conv = grad_conv.reshape(KW * CG, local_width)
    grad_start = grad_local + input_back.reshape(rows_here, local_width, length).transpose(0, 2, 1)
    input_grad = grad_start * (1.0 - masked)[..., None]
    grad_mask = jnp.sum(masked[..., None] * grad_start, axis=(0, 1))
    conv_done, query_done, key_done, value_done, out_done, up_done, down_done = (
        lax.psum_scatter(grad_conv, "dp", scatter_dimension=0, tiled=True),
        lax.psum_scatter(query_done, "dp", scatter_dimension=0, tiled=True),
        lax.psum_scatter(key_done, "dp", scatter_dimension=0, tiled=True),
        lax.psum_scatter(value_done, "dp", scatter_dimension=0, tiled=True),
        lax.psum_scatter(out_done, "dp", scatter_dimension=1, tiled=True),
        lax.psum_scatter(up_done, "dp", scatter_dimension=0, tiled=True),
        lax.psum_scatter(down_done, "dp", scatter_dimension=1, tiled=True),
    )
    summed = lax.psum(
        (
            grad_mask,
            grad_conv_bias,
            grad_query_bias,
            grad_value_bias,
            grad_out_bias,
            grad_gain_one,
            grad_shift_one,
            grad_up_bias,
            grad_down_bias,
            grad_gain_two,
            grad_shift_two,
            stats,
            frame_count,
        ),
        "dp",
    )
    stream_rms = jnp.sqrt(summed[11] / (summed[12] * width))
    return (
        layer_out,
        input_grad,
        summed[0],
        conv_done,
        summed[1],
        query_done,
        key_done,
        value_done,
        summed[2],
        summed[3],
        out_done,
        summed[4],
        summed[5],
        summed[6],
        up_done,
        summed[7],
        down_done,
        summed[8],
        summed[9],
        summed[10],
        stream_rms,
    )


def solution(mesh):
    placed = (
        P("dp", None, None),
        P("dp", None),
        P("dp", None),
        P(),
        P("dp", "mp"),
        P("mp"),
        P("dp", "mp"),
        P("dp", "mp"),
        P("dp", "mp"),
        P("mp"),
        P("mp"),
        P("mp", "dp"),
        P(),
        P(),
        P(),
        P("dp", "mp"),
        P("mp"),
        P("mp", "dp"),
        P(),
        P(),
        P(),
        P("dp", None, None),
    )
    return jax.shard_map(
        local,
        mesh=mesh,
        in_specs=placed,
        out_specs=(
            P("dp", None, None),
            P("dp", None, "mp"),
            P("mp"),
            P("dp", "mp"),
            P("mp"),
            P("dp", "mp"),
            P("dp", "mp"),
            P("dp", "mp"),
            P("mp"),
            P("mp"),
            P("mp", "dp"),
            P(),
            P(),
            P(),
            P("dp", "mp"),
            P("mp"),
            P("mp", "dp"),
            P(),
            P(),
            P(),
            P(),
        ),
        check_vma=False,
    )
```

profile of v0, /device:TPU:0, one launch (start us, length us, event | category | flops | bytes accessed | tf_op | source)
XLA Modules:
  0.0 1320.8 jit_solution(14473066164201392543)
XLA Ops:
  13.0 53.3 %all-gather.5.cloned.1.call-done = bf16[6144,384]{1,0:T(8,128)(2,1)} async-done(((bf16[384,384]{1,0:T(8,128)(2,1)}), bf16[6144,384]{1,0:T(8,128)(2,1)}) %all-gather.5.cloned.1.call-update) | async-done | bytes 4718608 | tf_op jit(solution)/shard_map/all_gather | solution.py:160
  66.3 17.1 %reshape.761 = bf16[128,48,8,48]{3,2,1,0:T(8,128)(2,1)} reshape(bf16[6144,384]{1,0:T(8,128)(2,1)} %all-gather.5.cloned.1.call-done) | data formatting | bytes 9437184 | tf_op jit(solution)/shard_map/reshape | solution.py:179
  83.4 13.7 %copy.94 = bf16[8,48,6144]{2,1,0:T(8,128)(2,1)} copy(bf16[8,48,6144]{1,0,2:T(8,128)(2,1)} %bitcast.524) | data formatting | bytes 9437184 | tf_op jit(solution)/shard_map/reshape | solution.py:180
  97.1 114.2 %while.78 = (s32[]{:T(128)}, f32[1,8,48,1024]{3,2,1,0:T(8,128)S(1)}, s32[8]{0:T(128)S(1)}, s32[1,1152]{1,0:T(1,128)S(1)}, s32[1,1024]{1,0:T(1,128)S(1)}, /*index...) while((s32[]{:T(128)}, ...), condition=%wide.region_1.2_spmd.clone, body=%wide.region_0.1_spmd.clone.sunk | while | flops 611074112 | bytes 66753808 | solution.py:198
  213.0 6.5 fusion.78
  220.9 20.6 %all_gather.26 = bf16[768,384]{1,0:T(8,128)(2,1)S(1)} all-gather(bf16[48,384]{1,0:T(8,128)(2,1)S(1)} %copy-done.53), channel_id=1, replica_groups=mesh['dp'=16,'mp'=2] {'dp'}, dimensions={0}, use_global_device_ids=true | all-gather | bytes 626688 | tf_op jit(solution)/shard_map/all_gather | solution.py:161
  241.5 20.4 %all_gather.27 = bf16[768,384]{1,0:T(8,128)(2,1)} all-gather(bf16[48,384]{1,0:T(8,128)(2,1)S(1)} %copy-done.54), channel_id=1, replica_groups=mesh['dp'=16,'mp'=2] {'dp'}, dimensions={0}, use_global_device_ids=true | all-gather | bytes 626688 | tf_op jit(solution)/shard_map/all_gather | solution.py:162
  261.9 21.9 %all_gather.28 = bf16[768,384]{1,0:T(8,128)(2,1)} all-gather(bf16[48,384]{1,0:T(8,128)(2,1)S(1)} %copy-done.55), channel_id=1, replica_groups=mesh['dp'=16,'mp'=2] {'dp'}, dimensions={0}, use_global_device_ids=true | all-gather | bytes 626688 | tf_op jit(solution)/shard_map/all_gather | solution.py:163
  283.8 20.4 %all_gather.29 = bf16[384,768]{0,1:T(8,128)(2,1)} all-gather(bf16[384,48]{0,1:T(8,128)(2,1)S(1)} %copy-done.56), channel_id=1, replica_groups=mesh['dp'=16,'mp'=2] {'dp'}, dimensions={1}, use_global_device_ids=true | all-gather | bytes 626688 | tf_op jit(solution)/shard_map/all_gather | solution.py:164
  313.1 52.7 %while.77 = (s32[]{:T(128)}, f32[2,512,6,64]{1,0,3,2:T(2,128)}, f32[2,6,512]{2,1,0:T(8,128)S(1)}, s32[2,512]{1,0:T(2,128)S(1)}, s32[1024]{0:T(1024)S(1)}, /*inde...) while((s32[]{:T(128)}, f32[2,512,6,64]{1,0,3,2:T(2,128)}, ...), condition=%wide.region_5.6_spmd, body=%wide.region_2.5_spmd.sunk | while | flops 843576320 | bytes 45865084 | solution.py:68
  324.8 15.0 %dynamic_update_slice.46 = f32[2,512,6,64]{1,0,3,2:T(2,128)} dynamic-update-slice(f32[2,512,6,64]{1,0,3,2:T(2,128)} %get-tuple-element.1357, f32[1,512,6,64]{1,0,3,2:T(1,128)S(1)} %copy.128, s32[]{:T(128)S(6)} %copy.190, s32[]{:T(128)} %constant.643.clone.1..sunk, s32[]{:T(128)} %constant.643.clone.1..sunk, s32[]{:T(128)} %constant.643.clone.1..sunk) | dynamic-update-slice | bytes 1572868 | tf_op jit(solution)/shard_map/while/body/eval_jaxpr/while/body/jit(dynamic_update_index_in_dim)/dynamic_update_slice | solution.py:68
  350.9 15.0 %dynamic_update_slice.46 = f32[2,512,6,64]{1,0,3,2:T(2,128)} dynamic-update-slice(f32[2,512,6,64]{1,0,3,2:T(2,128)} %get-tuple-element.1357, f32[1,512,6,64]{1,0,3,2:T(1,128)S(1)} %copy.128, s32[]{:T(128)S(6)} %copy.190, s32[]{:T(128)} %constant.643.clone.1..sunk, s32[]{:T(128)} %constant.643.clone.1..sunk, s32[]{:T(128)} %constant.643.clone.1..sunk) | dynamic-update-slice | bytes 1572868 | tf_op jit(solution)/shard_map/while/body/eval_jaxpr/while/body/jit(dynamic_update_index_in_dim)/dynamic_update_slice | solution.py:68
  377.4 48.8 %all-reduce.9.cloned.1.call-done = bf16[1024,768]{1,0:T(8,128)(2,1)} async-done(((bf16[1024,768]{1,0:T(8,128)(2,1)}), bf16[1024,768]{1,0:T(8,128)(2,1)}) %all-reduce.9.cloned.1.call-update) | async-done | bytes 1572880 | tf_op jit(solution)/shard_map/psum | solution.py:220
  432.4 38.6 %all-gather.9.cloned.1.call-done = bf16[768,1536]{1,0:T(8,128)(2,1)} async-done(((bf16[48,1536]{1,0:T(8,128)(2,1)}), bf16[768,1536]{1,0:T(8,128)(2,1)}) %all-gather.9.cloned.1.call-update) | async-done | bytes 2359312 | tf_op jit(solution)/shard_map/all_gather | solution.py:165
  471.0 19.9 %multiply_convert_fusion.1 = (bf16[1024,1536]{1,0:T(8,128)(2,1)}, f32[1024,1536]{1,0:T(8,128)}, f32[1024,1536]{1,0:T(8,128)}) fusion(f32[1536]{0:T(1024)S(1)} %convert_element_type.189, bf16[768,1536]{1,0:T(8,128)(2,1)} %all-gather.9.cloned.1.call-done, f32[1024,768]{1,0:T(8,128)} %copy-done.8, f32[768]{0:T(1024)S(1)} %convert_element_type.187, ...), kind=kOutput, calls=%fused_computation.204 | convolution fusion | flops 2523660288 | bytes 21254144 | tf_op jit(solution)/shard_map/dot_general | solution.py:26
  490.9 23.6 %all-gather.11.cloned.1.call-done = bf16[1536,768]{0,1:T(8,128)(2,1)} async-done(((bf16[1536,48]{0,1:T(8,128)(2,1)}), bf16[1536,768]{0,1:T(8,128)(2,1)}) %all-gather.11.cloned.1.call-update) | async-done | bytes 2359312 | tf_op jit(solution)/shard_map/all_gather | solution.py:166
  514.5 6.4 convolution_convert_fusion.2
  521.1 50.3 %all-reduce.11.cloned.1.call-done = bf16[1024,768]{1,0:T(8,128)(2,1)} async-done(((bf16[1024,768]{1,0:T(8,128)(2,1)}), bf16[1024,768]{1,0:T(8,128)(2,1)}) %all-reduce.11.cloned.1.call-update) | async-done | bytes 1572880 | tf_op jit(solution)/shard_map/psum | solution.py:230
  576.9 5.1 fusion.48
  586.6 5.1 convert_reduce_fusion
  597.2 51.5 %all-reduce.13.cloned.1.call-done = bf16[1024,768]{1,0:T(8,128)(2,1)} async-done(((bf16[1024,768]{1,0:T(8,128)(2,1)}), bf16[1024,768]{1,0:T(8,128)(2,1)}) %all-reduce.13.cloned.1.call-update) | async-done | bytes 1572880 | tf_op jit(solution)/shard_map/psum | solution.py:262
  648.8 4.9 multiply_reduce_fusion.2
  668.4 51.3 %while.79 = (s32[]{:T(128)}, f32[1024,6,64]{0,2,1:T(8,128)S(1)}, f32[1024,6,64]{0,2,1:T(8,128)}, bf16[2,512,6,64]{1,3,2,0:T(8,128)(2,1)}, bf16[2,512,6,64]{1,3,2...) while((s32[]{:T(128)}, f32[1024,6,64]{0,2,1:T(8,128)S(1)}, ...), condition=%wide.region_19.20_spmd.clone, body=%wide.region_17.19_spmd.clone.sunk | while | flops 2063332352 | bytes 144935232 | solution.py:121
  675.8 5.4 multiply_reduce_fusion.8
  681.1 5.1 multiply_convert_fusion.6
  686.3 5.9 fusion.193
  695.9 5.8 bitcast_add_fusion.13
  701.6 5.4 multiply_reduce_fusion.8
  707.0 5.1 multiply_convert_fusion.6
  712.1 5.9 fusion.193
  742.9 6.5 fusion.100
  749.4 14.6 %copy.91 = bf16[8,48,128,48]{3,2,1,0:T(8,128)(2,1)} copy(bf16[8,48,128,48]{3,0,1,2:T(8,128)(2,1)} %bitcast.525) | data formatting | bytes 9437184 | tf_op jit(solution)/shard_map/transpose | solution.py:311
  764.0 23.9 %reshape.776 = bf16[8,48,6144]{2,1,0:T(8,128)(2,1)} reshape(bf16[8,48,128,48]{3,2,1,0:T(8,128)(2,1)} %copy.91) | data formatting | bytes 9437184 | tf_op jit(solution)/shard_map/reshape | solution.py:311
  788.0 6.2 fusion.115
  804.2 360.0 %while.80 = (s32[]{:T(128)}, f32[1,8,48,1024]{3,2,1,0:T(8,128)S(1)}, f32[8,8,768,48]{2,3,1,0:T(8,128)}, s32[8]{0:T(128)S(1)}, s32[1,1152]{1,0:T(1,128)S(1)}, /*i...) while((s32[]{:T(128)}, ...), condition=%wide.region_22.23_spmd.clone, body=%wide.region_21.22_spmd.clone.sunk | while | flops 1221361792 | bytes 182069648 | solution.py:336
  824.6 6.3 copy.130
  834.5 5.2 copy.131
  839.6 9.7 fusion.198
  869.4 6.3 copy.130
  879.2 5.2 copy.131
  884.4 9.7 fusion.198
  914.0 6.4 copy.130
  924.0 5.2 copy.131
  929.2 9.6 fusion.198
  958.9 6.3 copy.130
  968.7 5.2 copy.131
  973.9 9.8 fusion.198
  1003.7 6.3 copy.130
  1013.6 5.2 copy.131
  1018.8 9.7 fusion.198
  1043.9 5.0 copy-done.3
  1048.9 6.5 copy.130
  1058.9 5.2 copy.131
  1064.2 9.7 fusion.198
  1093.8 6.3 copy.130
  1103.7 5.2 copy.131
  1108.9 9.6 fusion.198
  1138.5 6.9 copy.130
  1149.0 5.2 copy.131
  1154.1 9.9 fusion.198
  1164.2 16.7 %copy.95 = f32[8,8,768,48]{3,1,2,0:T(8,128)} copy(f32[8,8,768,48]{2,3,1,0:T(8,128)} %get-tuple-element.529) | data formatting | bytes 18874368 | tf_op jit(solution)/shard_map/reshape | solution.py:339
  1180.9 20.1 %reshape.779 = f32[6144,384]{1,0:T(8,128)} reshape(f32[8,16,48,8,48]{4,3,2,1,0:T(8,128)} %bitcast.526) | data formatting | bytes 18874368 | tf_op jit(solution)/shard_map/reshape | solution.py:342
  1208.8 64.7 %all-reduce.3 = (f32[384]{0:T(512)}, f32[384]{0:T(512)}, f32[384]{0:T(512)}, f32[384]{0:T(512)}, f32[768]{0:T(1024)}, /*index=5*/f32[768]{0:T(1024)}, f32[768]{0...) all-reduce(f32[384]{0:T(512)S(1)} %get-tuple-element.886, ...), channel_id=1, replica_groups=mesh['dp'=16,'mp'=2] {'dp'}, use_global_device_ids=true, to_apply=%region_24.25 | all-reduce | flops 7685 | bytes 61480 | tf_op jit(solution)/shard_map/psum | solution.py:355
  1274.7 39.3 %reduce-scatter.8.cloned.1.call-done = f32[384,384]{1,0:T(8,128)} async-done(((f32[6144,384]{1,0:T(8,128)}), f32[384,384]{1,0:T(8,128)}) %reduce-scatter.8.cloned.1.call-update) | async-done | bytes 589840 | tf_op jit(solution)/shard_map/reduce_scatter | solution.py:347
  (789 shorter events, 412.4 us)
Async XLA Ops:
  7.2 59.1 %all-gather.5.cloned.1.call-start = ((), (), s32[]{:S(2)}) async-start(), calls=%async_computation.7 | async-start | bytes 5013504 | tf_op jit(solution)/shard_map/all_gather | solution.py:160
  7.9 296.3 %all-gather.7.cloned.1.call-start = ((), (), s32[]{:S(2)}) async-start(), calls=%async_computation.8 | async-start | bytes 2359296 | tf_op jit(solution)/shard_map/all_gather | solution.py:205
  8.7 204.3 %copy-start.57 = (f32[384]{0:T(512)}, f32[384]{0:T(512)S(1)}, u32[]{:S(2)}) copy-start(f32[384]{0:T(512)S(1)} %convert_element_type.173) | copy-start | bytes 4612
  10.1 416.2 %copy-start.47 = (f32[1,1024]{1,0:T(1,128)}, f32[1,1024]{1,0:T(1,128)S(1)}, u32[]{:S(2)}) copy-start(f32[1,1024]{1,0:T(1,128)S(1)} %convert_element_type.170) | copy-start | bytes 12292
  12.9 584.3 %copy-start.43 = (f32[1,1024]{1,0:T(1,128)}, f32[1,1024]{1,0:T(1,128)S(1)}, u32[]{:S(2)}) copy-start(f32[1,1024]{1,0:T(1,128)S(1)} %compare_convert_fusion) | copy-start | bytes 12292
  211.3 8.2 copy-start
  211.3 8.2 copy-start.4
  212.9 6.7 copy-start.78
  212.9 6.7 copy-start.79
  212.9 7.9 copy-start.53
  212.9 28.5 %copy-start.54 = (bf16[48,384]{1,0:T(8,128)(2,1)S(1)}, bf16[48,384]{1,0:T(8,128)(2,1)}, u32[]{:S(2)}) copy-start(bf16[48,384]{1,0:T(8,128)(2,1)} %param.37) | copy-start | bytes 110596
  212.9 49.0 %copy-start.55 = (bf16[48,384]{1,0:T(8,128)(2,1)S(1)}, bf16[48,384]{1,0:T(8,128)(2,1)}, u32[]{:S(2)}) copy-start(bf16[48,384]{1,0:T(8,128)(2,1)} %param.38) | copy-start | bytes 110596
  213.0 70.8 %copy-start.56 = (bf16[384,48]{0,1:T(8,128)(2,1)S(1)}, bf16[384,48]{0,1:T(8,128)(2,1)}, u32[]{:S(2)}) copy-start(bf16[384,48]{0,1:T(8,128)(2,1)} %param.41) | copy-start | bytes 110596
  213.0 91.2 %copy-start.20 = (bf16[1,1024,768]{2,1,0:T(8,128)(2,1)S(1)}, bf16[1,1024,768]{2,1,0:T(8,128)(2,1)}, u32[]{:S(2)}) copy-start(bf16[1,1024,768]{2,1,0:T(8,128)(2,1)} %param.30) | copy-start | bytes 4718596
  219.6 206.7 %all-reduce.9.cloned.1.call-start = ((), (), s32[]{:S(2)}) async-start(), calls=%async_computation.9 | async-start | bytes 3145728 | tf_op jit(solution)/shard_map/psum | solution.py:220
  241.5 67.0 %copy-start.34 = (bf16[768,384]{1,0:T(8,128)(2,1)}, bf16[768,384]{1,0:T(8,128)(2,1)S(1)}, u32[]{:S(2)}) copy-start(bf16[768,384]{1,0:T(8,128)(2,1)S(1)} %all_gather.26) | copy-start | bytes 1769476
  365.9 6.5 copy-start.11
  365.9 6.5 copy-start.18
  365.9 6.5 copy-start.27
  372.4 4.9 copy-start.72
  372.4 4.9 copy-start.73
  372.4 4.9 copy-start.74
  372.4 4.9 copy-start.71
  376.1 94.9 %all-gather.9.cloned.1.call-start = ((), (), s32[]{:S(2)}) async-start(), calls=%async_computation.10 | async-start | bytes 2506752 | tf_op jit(solution)/shard_map/all_gather | solution.py:165
  376.6 137.9 %all-gather.11.cloned.1.call-start = ((), (), s32[]{:S(2)}) async-start(), calls=%async_computation.11 | async-start | bytes 2506752 | tf_op jit(solution)/shard_map/all_gather | solution.py:166
  377.2 194.1 %all-reduce.11.cloned.1.call-start = ((), (), s32[]{:S(2)}) async-start(), calls=%async_computation.12 | async-start | bytes 3145728 | tf_op jit(solution)/shard_map/psum | solution.py:230
  377.3 276.3 %copy-start.49 = (f32[768]{0:T(1024)}, f32[768]{0:T(1024)S(1)}, u32[]{:S(2)}) copy-start(f32[768]{0:T(1024)S(1)} %convert_element_type.186) | copy-start | bytes 9220
  377.3 194.0 %copy-start.60 = (f32[768]{0:T(1024)}, f32[768]{0:T(1024)S(1)}, u32[]{:S(2)}) copy-start(f32[768]{0:T(1024)S(1)} %convert_element_type.187) | copy-start | bytes 9220
  430.1 223.5 %copy-start.45 = (f32[1024]{0:T(1024)}, f32[1024]{0:T(1024)S(1)}, u32[]{:S(2)}) copy-start(f32[1024]{0:T(1024)S(1)} %broadcast_multiply_fusion.2) | copy-start | bytes 12292
  432.4 221.3 %copy-start.51 = (f32[1024]{0:T(1024)}, f32[1024]{0:T(1024)S(1)}, u32[]{:S(2)}) copy-start(f32[1024]{0:T(1024)S(1)} %fusion.94) | copy-start | bytes 12292
  514.5 6.5 copy-start.75
  514.5 6.5 copy-start.76
  514.5 6.5 copy-start.77
  521.0 127.8 %all-reduce.13.cloned.1.call-start = ((), (), s32[]{:S(2)}) async-start(), calls=%async_computation.13 | async-start | bytes 3145728 | tf_op jit(solution)/shard_map/psum | solution.py:262
  576.8 9.5 slice-start
  576.8 9.5 slice-start.2
  586.3 5.3 copy-start.40
  586.6 6.8 copy-start.80
  597.1 197.2 %all-reduce.15.cloned.1.call-start = ((), (), s32[]{:S(2)}) async-start(), calls=%async_computation.14 | async-start | bytes 3145728 | tf_op jit(solution)/shard_map/psum | solution.py:302
  648.8 4.9 copy-start.9
  648.8 5.2 copy-start.17
  648.8 5.6 copy-start.23
  660.6 7.8 copy-start.12
  686.2 5.9 copy-start.2
  686.3 5.9 copy-start.13
  712.1 5.9 copy-start.2
  712.1 5.9 copy-start.13
  719.8 5.9 copy-start.32
  719.8 4.9 copy-start.38
  729.1 545.6 %reduce-scatter.16.cloned.1.call-start = ((), (), s32[]{:S(2)}) async-start(), calls=%async_computation.19 | async-start | bytes 1253376 | tf_op jit(solution)/shard_map/reduce_scatter | solution.py:351
  732.8 541.9 %reduce-scatter.14.cloned.1.call-start = ((), (), s32[]{:S(2)}) async-start(), calls=%async_computation.18 | async-start | bytes 1253376 | tf_op jit(solution)/shard_map/reduce_scatter | solution.py:350
  736.7 538.0 %reduce-scatter.12.cloned.1.call-start = ((), (), s32[]{:S(2)}) async-start(), calls=%async_computation.17 | async-start | bytes 1253376 | tf_op jit(solution)/shard_map/reduce_scatter | solution.py:349
  738.9 535.8 %reduce-scatter.10.cloned.1.call-start = ((), (), s32[]{:S(2)}) async-start(), calls=%async_computation.16 | async-start | bytes 1253376 | tf_op jit(solution)/shard_map/reduce_scatter | solution.py:348
  742.8 531.9 %reduce-scatter.18.cloned.1.call-start = ((), (), s32[]{:S(2)}) async-start(), calls=%async_computation.20 | async-start | bytes 5013504 | tf_op jit(solution)/shard_map/reduce_scatter | solution.py:352
  749.4 525.4 %reduce-scatter.20.cloned.1.call-start = ((), (), s32[]{:S(2)}) async-start(), calls=%async_computation.21 | async-start | bytes 5013504 | tf_op jit(solution)/shard_map/reduce_scatter | solution.py:353
  764.0 23.9 %copy-start.41 = (bf16[1024,768]{1,0:T(8,128)(2,1)S(1)}, bf16[1024,768]{1,0:T(8,128)(2,1)}, u32[]{:S(2)}) copy-start(bf16[1024,768]{1,0:T(8,128)(2,1)} %copy-done.40) | copy-start | bytes 4718596
  794.2 519.9 %reduce-scatter.8.cloned.1.call-start = ((), (), s32[]{:S(2)}) async-start(), calls=%async_computation.15 | async-start | bytes 10027008 | tf_op jit(solution)/shard_map/reduce_scatter | solution.py:347
  820.0 4.6 copy-start.3
  864.8 4.6 copy-start.3
  909.5 4.6 copy-start.3
  954.3 4.6 copy-start.3
  999.2 4.6 copy-start.3
  1043.9 5.0 copy-start.3
  1089.2 4.6 copy-start.3
  (50 other events, 145.8 us)
Sparse Core Ops, SparseCore 0:
  10.3 55.9 all-gather.4
  219.7 25.7 all-gather.6
  376.2 49.9 all-reduce.8
  428.6 42.3 all-gather.8
  473.4 41.0 all-gather.10
  521.1 50.2 all-reduce.10
  597.2 51.4 all-reduce.12
  729.2 51.4 all-reduce.14
  784.9 58.1 reduce-scatter.15
  847.1 57.0 reduce-scatter.13
  908.4 57.1 reduce-scatter.11
  969.6 57.1 reduce-scatter.9
  1031.2 74.6 reduce-scatter.17
  1110.6 74.6 reduce-scatter.19
  1201.2 112.8 reduce-scatter.7
where the time goes:
time: 1340 us; the launch traced here: 1320 us
  local copies, waits for them, and re-layouts  330 us (25%)
  waiting for transfers between devices  308 us (23%)
  matrix products  261 us (19%)
  other arithmetic  230 us (17%)
  blocking collectives  148 us (11%)
  loops' own time  28 us (2%)
  between operations  15.9 us (1%)
    while x360, other arithmetic  139 us
    another operation x24, local copies, waits for them, and re-layouts, masked_taps(): stacked = jnp.stack(pieces, axis=2)  109 us
    dot_general x8, matrix products, conv_back_step(): jnp.einsum('rgmt,rgot->gmo', patches, grad_chan, preferred_element_type=j...  77.8 us
    psum x1, blocking collectives, local(): lax.psum((grad_mask, grad_conv_bias, grad_query_bias, grad_value_bias, gr...  64.7 us
    all_gather x1, waiting for transfers between devices, local(): lax.all_gather(conv_weight, 'dp', axis=0, tiled=True)  53.3 us
    psum x1, waiting for transfers between devices, local(): lax.psum(jnp.einsum('nf,df->nd', hidden_grad, up_back, preferred_element_...  51.5 us
    psum x1, waiting for transfers between devices, local(): lax.psum(matmul(hidden_low, down_full).astype(jnp.bfloat16), 'mp')  50.3 us
    psum x1, waiting for transfers between devices, local(): lax.psum(matmul(ctx_low, out_full).astype(jnp.bfloat16), 'mp')  48.8 us
  transfers between devices with their start and end apart: 15, of which 7 were waited for; matrix products, arithmetic and copies ran while one was open for 35% of the time, Pallas kernels for 0%

commit v1 on v0

v1 whole, which is shorter than its diff:
```python
import functools

import jax
import jax.numpy as jnp
from jax import lax
from jax.experimental import pallas as pl
from jax.experimental.pallas import tpu as pltpu
from jax.sharding import PartitionSpec as P

HD = 64
KW = 128
CG = 48
TAPS = 8
EPS = 1e-05
F32 = jnp.float32
BF16 = jnp.bfloat16
NN = (((1,), (0,)), ((), ()))
NT = (((1,), (1,)), ((), ()))
TN = (((0,), (0,)), ((), ()))
BOTH = ("dp", "mp")


def dg(a, b, dims):
    return lax.dot_general(a, b, dims, preferred_element_type=F32)


def gelu_parts(v):
    t = 1.0 / (1.0 + (0.3275911 * 0.7071067811865476) * jnp.abs(v))
    e = jnp.exp(-0.5 * v * v)
    poly = t * (0.254829592 + t * (-0.284496736 + t * (1.421413741 + t * (-1.453152027 + t * 1.061405429))))
    tail = 0.5 * poly * e
    return jnp.where(v >= 0, 1.0 - tail, tail), e


def gelu_and_slope(v):
    phi, e = gelu_parts(v)
    return v * phi, phi + v * e * 0.3989422804014327


def params(mb=56):
    return pltpu.CompilerParams(vmem_limit_bytes=mb * 2**20)


def vspec():
    return pl.BlockSpec(memory_space=pltpu.VMEM)


def call(kernel, outs, scratch, *args):
    return pl.pallas_call(
        kernel,
        out_shape=[jax.ShapeDtypeStruct(s, d) for s, d in outs],
        in_specs=[vspec()] * len(args),
        out_specs=[vspec()] * len(outs),
        scratch_shapes=[pltpu.VMEM(s, d) for s, d in scratch],
        compiler_params=params(),
    )(*args)


def split_low(v):
    hi = v.astype(BF16)
    return hi, (v - hi.astype(F32)).astype(BF16)


def spread_matrix(seg, length, width):
    rank = jnp.where(seg == 0, 7, seg - 1)
    pos = lax.broadcasted_iota(jnp.int32, (length, 1), 0) + 64 * rank + 8
    hit = pos == lax.broadcasted_iota(jnp.int32, (length, width), 1)
    return hit.astype(F32).astype(BF16)


def rolled(x, left):
    width = x.shape[1]
    left = left % width
    return x if left == 0 else pltpu.roll(x, width - left, 1)


def tap_patches(xg):
    return jnp.concatenate([rolled(xg, r) for r in range(TAPS)], axis=0)


def conv_fwd_kernel(seg_ref, x_ref, w_ref, b_ref, low_ref, slope_ref, spread, xq, y_ref, ot):
    length, width = spread.shape
    blocks = w_ref.shape[0]
    spread[...] = spread_matrix(seg_ref[...], length, width)
    xq[...] = dg(x_ref[...], spread[...], TN).astype(BF16)

    def body(g, carry):
        at = pl.ds(pl.multiple_of(g * CG, 16), CG)
        y_ref[...] = dg(w_ref[:, at, :].reshape(blocks * CG, TAPS * CG), tap_patches(xq[at, :]), NN)
        acc = rolled(y_ref[0:CG, :], -64)
        for b in range(1, blocks):
            acc = acc + rolled(y_ref[b * CG:(b + 1) * CG, :], TAPS * b - 64)
        ot[at, :] = acc
        return carry

    lax.fori_loop(0, x_ref.shape[1] // CG, body, 0)
    hi, lo = split_low(ot[...])
    pre = dg(spread[...], hi, NT) + dg(spread[...], lo, NT) + b_ref[...]
    valid = (seg_ref[...] != 0).astype(F32)
    value, slope = gelu_and_slope(pre)
    low_ref[...] = (valid * value).astype(BF16)
    slope_ref[...] = valid * slope


def conv_bwd_kernel(seg_ref, x_ref, w_ref, slope_ref, gm_ref, mask_ref, dw_ref, in_ref, db_ref, dm_ref,
                    spread, xq, dq, d_ref, gq):
    length, width = spread.shape
    blocks = w_ref.shape[0]
    spread[...] = spread_matrix(seg_ref[...], length, width)
    xq[...] = dg(x_ref[...], spread[...], TN).astype(BF16)
    dpre = (slope_ref[...] * gm_ref[...].astype(F32)).astype(BF16)
    db_ref[...] = jnp.sum(dpre.astype(F32), axis=0, keepdims=True)
    dq[...] = dg(dpre, spread[...], TN).astype(BF16)

    def body(g, carry):
        at = pl.ds(pl.multiple_of(g * CG, 16), CG)
        dqg = dq[at, :]
        for b in range(blocks):
            d_ref[b * CG:(b + 1) * CG, :] = rolled(dqg, 64 - TAPS * b)
        dmat = d_ref[...]
        dw = dg(dmat, tap_patches(xq[at, :]), NT)
        dw_ref[:, at, :] = dw.astype(dw_ref.dtype).reshape(blocks, CG, TAPS * CG)
        v = dg(w_ref[:, at, :].reshape(blocks * CG, TAPS * CG), dmat, TN)
        acc = v[0:CG, :]
        for r in range(1, TAPS):
            acc = acc + rolled(v[r * CG:(r + 1) * CG, :], -r)
        gq[at, :] = acc
        return carry

    lax.fori_loop(0, x_ref.shape[1] // CG, body, 0)
    hi, lo = split_low(gq[...])
    grad = dg(spread[...], hi, NT) + dg(spread[...], lo, NT) + gm_ref[...].astype(F32)
    masked = mask_ref[...].astype(F32)
    dm_ref[...] = jnp.sum(masked * grad, axis=0, keepdims=True)
    in_ref[...] = (1.0 - masked) * grad


def attn_fwd_kernel(hid_ref, c0_ref, c1_ref, mask_ref, segc_ref, segr_ref, emb_ref, w_ref, qb_ref, vb_ref,
                    mixed_ref, mlow_ref, qkv_ref, ctx_ref, lse_ref, part_ref, stat_ref, qt, vt, ot):
    rows, width = hid_ref.shape
    half = c0_ref.shape[1]
    heads = half // HD
    step = 256
    stat = jnp.zeros((1, half), F32)
    for i in range(rows // step):
        at = pl.ds(i * step, step)
        conv = jnp.concatenate([c0_ref[at, :].astype(F32), c1_ref[at, :].astype(F32)], axis=1)
        hid = hid_ref[at, :].astype(F32)
        masked = mask_ref[at, :].astype(F32)
        mixed = hid + masked * (emb_ref[...] - hid) + conv
        low = mixed.astype(BF16)
        mixed_ref[at, :] = mixed
        mlow_ref[at, :] = low
        stat = stat + jnp.sum(conv[:, :half] * conv[:, :half] + conv[:, half:] * conv[:, half:], axis=0, keepdims=True)
        qkv = dg(low, w_ref[:, :3 * half], NN)
        qkv_ref[at, 0:half] = (qkv[:, :half] + qb_ref[...]).astype(BF16)
        qkv_ref[at, half:2 * half] = qkv[:, half:2 * half].astype(BF16)
        qkv_ref[at, 2 * half:] = (qkv[:, 2 * half:] + vb_ref[...]).astype(BF16)
    stat_ref[...] = stat
    qt[...] = (qkv_ref[:, 0:half] * jnp.asarray(HD ** -0.5, BF16)).T
    vt[...] = qkv_ref[:, 2 * half:].T

    def pair_body(p, carry):
        lanes = pl.ds(pl.multiple_of(half + p * 128, 128), 128)
        k_pair = qkv_ref[:, lanes]
        for j in range(2):
            head_at = pl.ds(pl.multiple_of(p * 128 + j * HD, HD), HD)
            qh = qt[head_at, :]
            vh = vt[head_at, :]
            zero = jnp.zeros_like(qh)
            qz = jnp.concatenate([qh, zero] if j == 0 else [zero, qh], axis=0)
            for i in range(rows // step):
                at = slice(i * step, (i + 1) * step)
                s = dg(k_pair, qz[:, at], NN)
                s = jnp.where(segc_ref[...] == segr_ref[:, at], s, -1000000000.0)
                top = jnp.max(s, axis=0, keepdims=True)
                e = jnp.exp(s - top)
                den = jnp.sum(e, axis=0, keepdims=True)
                o = dg(vh, e.astype(BF16), NN) / den
                ot[head_at, at] = jnp.where(segr_ref[:, at] != 0, o, 0.0).astype(BF16)
                lse_ref[pl.ds(2 * p + j, 1), at] = top + jnp.log(den)
        return carry

    lax.fori_loop(0, heads // 2, pair_body, 0)
    ctx_ref[...] = ot[...].T
    part_ref[...] = dg(ctx_ref[...], w_ref[:, 3 * half:], NT).astype(BF16)


def norm_stats(x):
    centre = x - jnp.mean(x, axis=-1, keepdims=True)
    r = lax.rsqrt(jnp.mean(centre * centre, axis=-1, keepdims=True) + EPS)
    return centre * r, r


def ffn_fwd_kernel(mixed_ref, p0_ref, p1_ref, seg_ref, ob_ref, g1_ref, s1_ref, up_ref, ub_ref, dt_ref,
                   n1_ref, r1_ref, low_ref, hid_ref, slope_ref, part_ref, stat_ref):
    rows, width = mixed_ref.shape
    step = 256
    stat_ref[...] = jnp.zeros_like(stat_ref)

    def body(i, carry):
        at = pl.ds(pl.multiple_of(i * step, step), step)
        attn = ob_ref[...] + (p0_ref[at, :].astype(F32) + p1_ref[at, :].astype(F32))
        valid = (seg_ref[at, :] != 0).astype(F32)
        stat_ref[...] += jnp.sum(valid * attn * attn, axis=0, keepdims=True)
        n1, r1 = norm_stats(mixed_ref[at, :] + attn)
        n1_ref[at, :] = n1
        r1_ref[at, :] = r1
        low = (n1 * g1_ref[...] + s1_ref[...]).astype(BF16)
        low_ref[at, :] = low
        pre = dg(low, up_ref[...], NN) + ub_ref[...]
        value, slope = gelu_and_slope(pre)
        hidden = value.astype(BF16)
        hid_ref[at, :] = hidden
        slope_ref[at, :] = slope.astype(BF16)
        part_ref[at, :] = dg(hidden, dt_ref[...], NT).astype(BF16)
        return carry

    lax.fori_loop(0, rows // step, body, 0)


def norm_back(gn, n, r):
    return r * (gn - jnp.mean(gn, axis=-1, keepdims=True) - n * jnp.mean(gn * n, axis=-1, keepdims=True))


def ffn_bwd_kernel(n1_ref, g1_ref, s1_ref, p0_ref, p1_ref, seg_ref, db_ref, g2_ref, s2_ref, cot_ref, low_ref,
                   hid_ref, slope_ref, up_ref, dt_ref,
                   out_ref, gr2_ref, part_ref, ddt_ref, dup_ref, sums_ref, dub_ref, fg, hg):
    rows, width = n1_ref.shape
    step = 256
    sums_ref[...] = jnp.zeros_like(sums_ref)
    dub_ref[...] = jnp.zeros_like(dub_ref)

    def body(i, carry):
        at = pl.ds(pl.multiple_of(i * step, step), step)
        ffn = db_ref[...] + (p0_ref[at, :].astype(F32) + p1_ref[at, :].astype(F32))
        valid = (seg_ref[at, :] != 0).astype(F32)
        resid = n1_ref[at, :] * g1_ref[...] + s1_ref[...] + ffn
        n2, r2 = norm_stats(resid)
        final = valid * (n2 * g2_ref[...] + s2_ref[...])
        out_ref[at, :] = final.astype(BF16)
        gf = valid * cot_ref[at, :].astype(F32)
        gr2 = norm_back(gf * g2_ref[...], n2, r2)
        gr2_ref[at, :] = gr2
        ffn_grad = gr2.astype(BF16)
        fg[at, :] = ffn_grad
        row_sum = lambda v: jnp.sum(v, axis=0, keepdims=True)
        sums_ref[...] += jnp.concatenate(
            [row_sum(valid * ffn * ffn), row_sum(final * final), row_sum(gf * n2), row_sum(gf), row_sum(ffn_grad.astype(F32))], axis=0)
        gh = dg(ffn_grad, dt_ref[...], NN)
        hidden_grad = (slope_ref[at, :].astype(F32) * gh).astype(BF16)
        hg[at, :] = hidden_grad
        dub_ref[...] += row_sum(hidden_grad.astype(F32))
        part_ref[at, :] = dg(hidden_grad, up_ref[...], NT).astype(BF16)
        return carry

    lax.fori_loop(0, rows // step, body, 0)
    ddt_ref[...] = dg(fg[...], hid_ref[...], TN).astype(ddt_ref.dtype)
    dup_ref[...] = dg(low_ref[...], hg[...], TN).astype(dup_ref.dtype)


def attn_bwd_kernel(gr2_ref, p0_ref, p1_ref, n1_ref, r1_ref, g1_ref, segc_ref, segr_ref, ctx_ref, qkv_ref, lse_ref,
                    mlow_ref, w_ref,
                    own_ref, send_ref, dw_ref, sums_ref, dqkvb_ref, gr1, cg, qt, kt, ct, dqt, dk, dv, gqkv):
    rows, width = gr2_ref.shape
    half = ctx_ref.shape[1]
    heads = half // HD
    step = 256
    core = lax.rem(lax.axis_index("dp"), 2)
    sums_ref[...] = jnp.zeros_like(sums_ref)
    row_sum = lambda v: jnp.sum(v, axis=0, keepdims=True)

    def norm_body(i, carry):
        at = pl.ds(pl.multiple_of(i * step, step), step)
        gn1 = gr2_ref[at, :] + (p0_ref[at, :].astype(F32) + p1_ref[at, :].astype(F32))
        n1 = n1_ref[at, :]
        g = norm_back(gn1 * g1_ref[...], n1, r1_ref[at, :])
        gr1[at, :] = g
        attn_grad = g.astype(BF16)
        sums_ref[...] += jnp.concatenate([row_sum(gn1 * n1), row_sum(gn1), row_sum(attn_grad.astype(F32))], axis=0)
        back = dg(attn_grad, w_ref[:, 3 * half:], NN)
        cg[at, :] = jnp.where(segc_ref[at, :] != 0, back, 0.0).astype(BF16)
        return carry

    lax.fori_loop(0, rows // step, norm_body, 0)
    dw_ref[:, 3 * half:] = dg(gr1[...].astype(BF16), ctx_ref[...], TN).astype(dw_ref.dtype)
    scale = jnp.asarray(HD ** -0.5, BF16)
    qt[...] = (qkv_ref[:, 0:half] * scale).T
    kt[...] = qkv_ref[:, half:2 * half].T
    ct[...] = cg[...].T
    lane = lax.broadcasted_iota(jnp.int32, (1, 128), 1)

    def pair_body(p, carry):
        base = pl.multiple_of(p * 128, 128)
        k_at = pl.ds(pl.multiple_of(half + base, 128), 128)
        v_at = pl.ds(pl.multiple_of(2 * half + base, 128), 128)
        q_pair = qkv_ref[:, pl.ds(base, 128)] * scale
        o_pair = cg[:, pl.ds(base, 128)]
        dk[...] = jnp.zeros_like(dk)
        dv[...] = jnp.zeros_like(dv)
        for j in range(2):
            head_at = pl.ds(pl.multiple_of(base + j * HD, HD), HD)
            zero = jnp.zeros((HD, rows), BF16)
            put = lambda a: jnp.concatenate([a, zero] if j == 0 else [zero, a], axis=0)
            qz, cz, kh = put(qt[head_at, :]), put(ct[head_at, :]), kt[head_at, :]
            keep = (lane < HD) if j == 0 else (lane >= HD)
            for i in range(rows // step):
                at = slice(i * step, (i + 1) * step)
                s = dg(qkv_ref[:, k_at], qz[:, at], NN)
                pr = jnp.exp(s - lse_ref[pl.ds(2 * p + j, 1), at])
                pr = jnp.where(segc_ref[...] == segr_ref[:, at], pr, 0.0)
                gp = dg(qkv_ref[:, v_at], cz[:, at], NN)
                delta = jnp.sum(pr * gp, axis=0, keepdims=True)
                ds = (pr * (gp - delta)).astype(BF16)
                dv[...] += dg(pr.astype(BF16), jnp.where(keep, o_pair[at, :], jnp.zeros_like(o_pair[at, :])), NN)
                dk[...] += dg(ds, jnp.where(keep, q_pair[at, :], jnp.zeros_like(q_pair[at, :])), NN)
                dqt[head_at, at] = (dg(kh, ds, NN) * (HD ** -0.5)).astype(BF16)
        gqkv[:, k_at] = dk[...].astype(BF16)
        gqkv[:, v_at] = dv[...].astype(BF16)
        return carry

    lax.fori_loop(0, heads // 2, pair_body, 0)
    gqkv[:, 0:half] = dqt[...].T
    dqkvb_ref[...] = row_sum(gqkv[...].astype(F32))
    dw_ref[:, :3 * half] = dg(mlow_ref[...], gqkv[...], TN).astype(dw_ref.dtype)
    mine = pl.ds(pl.multiple_of(core * half, 128), half)
    other = pl.ds(pl.multiple_of((1 - core) * half, 128), half)
    own_ref[...] = gr1[:, mine] + dg(gqkv[...], w_ref[mine, 0:3 * half], NT)
    send_ref[...] = dg(gqkv[...], w_ref[other, 0:3 * half], NT).astype(BF16)


def local(n_dp, hidden_in, segment_ids, time_mask, mask_embed, conv_weight, conv_bias, query_weight, key_weight,
          value_weight, query_bias, value_bias, out_weight, out_bias, first_gain, first_shift, up_weight, up_bias,
          down_weight, down_bias, second_gain, second_shift, cotangent):
    _, rows, width = hidden_in.shape
    half = width // 2
    ff = up_weight.shape[1]
    spread_width = -(-(rows + 7 * 64 + 64) // 128) * 128
    blocks = KW // TAPS
    part = lax.axis_index("mp")
    core = lax.rem(lax.axis_index("dp"), 2)
    n_all = 2 * n_dp
    turn = [(f, f // 4 * 4 + (f % 2) * 2 + (f // 2) % 2) for f in range(n_all)]
    sibling = [(f, f ^ 2) for f in range(n_all)]
    core_groups = [[f for f in range(n_all) if (f // 2) % 2 == c] for c in range(2)]
    swap = lambda v: lax.ppermute(v, BOTH, sibling)
    turned = lambda v: lax.ppermute(v, BOTH, turn)
    mine = part == core

    if conv_weight.shape[0] == TAPS * CG:
        conv_full = lax.all_gather(conv_weight.T, "dp", axis=0, tiled=True)
        conv_full = conv_full.reshape(blocks, half, TAPS * CG)
    else:
        conv_full = lax.all_gather(conv_weight, "dp", axis=0, tiled=True)
        conv_full = conv_full.reshape(blocks, TAPS * CG, half).swapaxes(1, 2)
    wall = jnp.concatenate([query_weight, key_weight, value_weight, out_weight.T, up_weight, down_weight.T], axis=1)
    wall = lax.all_gather(turned(wall), BOTH, axis=0, tiled=True, axis_index_groups=core_groups)
    w_qkvo, w_up, w_down = wall[:, :4 * half], wall[:, 4 * half:4 * half + ff], wall[:, 4 * half + ff:]
    bias = turned(jnp.concatenate([query_bias, value_bias, up_bias])[None])
    qb, vb, ub = (b.astype(F32) for b in (bias[:, :half], bias[:, half:2 * half], bias[:, 2 * half:]))
    row = lambda v: v.astype(F32)[None]

    hid, cot = hidden_in[0], cotangent[0]
    small = jnp.concatenate([segment_ids, time_mask], axis=0)
    hid_s = jnp.where(mine, hid, swap(hid))
    cot_s = jnp.where(mine, cot, swap(cot))
    small_s = jnp.where(mine, small, swap(small))
    seg_c, mask_c = segment_ids.reshape(rows, 1), time_mask.reshape(rows, 1)
    seg_sr, seg_sc, mask_sc = small_s[0:1], small_s[0].reshape(rows, 1), small_s[1].reshape(rows, 1)

    masked = mask_c.astype(F32)
    hid_half = lax.dynamic_slice_in_dim(hid, part * half, half, 1).astype(F32)
    emb_half = lax.dynamic_slice_in_dim(mask_embed, part * half, half, 0).astype(F32)
    start_half = (hid_half + masked * (emb_half - hid_half)).astype(BF16)
    conv_low, conv_slope = call(
        conv_fwd_kernel, [((rows, half), BF16), ((rows, half), F32)],
        [((rows, spread_width), BF16), ((half, spread_width), BF16), ((blocks * CG, spread_width), F32), ((half, spread_width), F32)],
        seg_c, start_half, conv_full, row(conv_bias))
    conv_s = turned(conv_low)
    conv_o = swap(conv_s)
    c0, c1 = jnp.where(core == 0, conv_s, conv_o), jnp.where(core == 0, conv_o, conv_s)

    heads = half // HD
    mixed, mlow, qkv, ctx, lse, part1, stat_conv = call(
        attn_fwd_kernel,
        [((rows, width), F32), ((rows, width), BF16), ((rows, 3 * half), BF16), ((rows, half), BF16), ((heads, rows), F32), ((rows, width), BF16), ((1, half), F32)],
        [((half, rows), BF16)] * 3,
        hid_s, c0, c1, mask_sc, seg_sc, seg_sr, row(mask_embed), w_qkvo, qb, vb)
    n1, r1, nlow, hidden, slope, part2, stat_attn = call(
        ffn_fwd_kernel,
        [((rows, width), F32), ((rows, 1), F32), ((rows, width), BF16), ((rows, ff), BF16), ((rows, ff), BF16), ((rows, width), BF16), ((1, width), F32)],
        [],
        mixed, part1, swap(part1), seg_sc, row(out_bias), row(first_gain), row(first_shift), w_up, ub, w_down)
    out_s, gr2, part3, d_down, d_up, sums2, d_ub = call(
        ffn_bwd_kernel,
        [((rows, width), BF16), ((rows, width), F32), ((rows, width), BF16), ((width, ff), BF16), ((width, ff), BF16), ((5, width), F32), ((1, ff), F32)],
        [((rows, width), BF16), ((rows, ff), BF16)],
        n1, row(first_gain), row(first_shift), part2, swap(part2), seg_sc, row(down_bias), row(second_gain), row(second_shift), cot_s, nlow,
        hidden, slope, w_up, w_down)
    other_out = lax.ppermute(out_s, "mp", [(0, 1), (1, 0)])
    layer_out = jnp.where(mine, out_s, other_out)[None]
    own, send, d_qkvo, sums1, d_qkvb = call(
        attn_bwd_kernel,
        [((rows, half), F32), ((rows, half), BF16), ((width, 4 * half), BF16), ((3, width), F32), ((1, 3 * half), F32)],
        [((rows, width), F32), ((rows, half), BF16), ((half, rows), BF16), ((half, rows), BF16), ((half, rows), BF16), ((half, rows), BF16),
         ((rows, 128), F32), ((rows, 128), F32), ((rows, 3 * half), BF16)],
        gr2, part3, swap(part3), n1, r1, row(first_gain), seg_sc, seg_sr, ctx, qkv, lse, mlow, w_qkvo)
    gm_half = turned((own + swap(send).astype(F32)).astype(BF16))
    d_conv, input_grad, d_cb, d_me = call(
        conv_bwd_kernel,
        [((blocks, half, TAPS * CG), BF16), ((rows, half), F32), ((1, half), F32), ((1, half), F32)],
        [((rows, spread_width), BF16), ((half, spread_width), BF16), ((half, spread_width), BF16), ((blocks * CG, spread_width), BF16), ((half, spread_width), F32)],
        seg_c, start_half, conv_full, conv_slope, gm_half, mask_c)

    d_wall = jnp.concatenate([d_qkvo, d_up, d_down], axis=1)
    d_wall = turned(lax.psum_scatter(d_wall, BOTH, scatter_dimension=0, tiled=True, axis_index_groups=core_groups)).astype(F32)
    if conv_weight.shape[0] == TAPS * CG:
        d_conv = lax.psum_scatter(d_conv.reshape(blocks * half, TAPS * CG), "dp", scatter_dimension=0, tiled=True).T.astype(F32)
    else:
        d_conv = lax.psum_scatter(d_conv.swapaxes(1, 2).reshape(blocks * TAPS * CG, half), "dp", scatter_dimension=0, tiled=True).astype(F32)
    once = (jnp.arange(width) // half == core).astype(F32)[None]
    put = lambda v, which: lax.dynamic_update_slice(jnp.zeros((1, 2 * v.shape[1]), F32), v, (0, which * v.shape[1]))
    full = jnp.concatenate([sums2, sums1, stat_attn], axis=0) * once
    pieces = [put(d_me, part), put(d_cb, part), put(d_qkvb[:, :half], core), put(d_qkvb[:, 2 * half:], core), put(d_ub, core)]
    stats = jnp.stack([jnp.sum(stat_conv) * 0.5, jnp.sum(full[8]), jnp.sum(full[0]), jnp.sum(full[1]), jnp.sum((seg_c != 0).astype(F32)) * 0.5])
    flat = jnp.concatenate([jnp.concatenate(pieces, axis=1)[0], full[2:8].reshape(-1), stats])
    flat = lax.psum(flat, BOTH)
    at = 0
    sections = []
    for size in (width, width, width, width, 2 * ff) + (width,) * 6 + (5,):
        sections.append(flat[at:at + size])
        at += size
    me, cb, dqb, dvb, dub, g2, s2, db, g1, s1, ob, st = sections
    half_of = lambda v: lax.dynamic_slice_in_dim(v, part * (v.shape[0] // 2), v.shape[0] // 2, 0)
    stream_rms = jnp.sqrt(st[:4] / (st[4] * width))
    q_, k_, v_, o_, u_, d_ = jnp.split(d_wall, [half, 2 * half, 3 * half, 4 * half, 4 * half + ff], axis=1)
    return (layer_out, input_grad[None], half_of(me), d_conv, half_of(cb), q_, k_, v_, half_of(dqb), half_of(dvb), o_.T, ob, g1, s1,
            u_, half_of(dub), d_.T, db, g2, s2, stream_rms)


def solution(mesh):
    split, half, turn = P("dp", "mp"), P("mp"), P("mp", "dp")
    whole = P()
    rows = P("dp", None, None)
    return jax.shard_map(
        functools.partial(local, mesh.shape["dp"]),
        mesh=mesh,
        in_specs=(rows, P("dp", None), P("dp", None), whole, split, half, split, split, split, half, half, turn, whole, whole, whole,
                  split, half, turn, whole, whole, whole, rows),
        out_specs=(rows, P("dp", None, "mp"), half, split, half, split, split, split, half, half, turn, whole, whole, whole,
                   split, half, turn, whole, whole, whole, whole),
        check_vma=False,
    )
```

time: 1340 us -> 570 us (0.43)
  local copies, waits for them, and re-layouts: 330 us -> 44.7 us
  matrix products: 261 us -> 0 us
  other arithmetic: 230 us -> 17.8 us
  Pallas kernels: 0 us -> 173 us
  blocking collectives: 148 us -> 41.4 us
  waiting for transfers between devices: 308 us -> 224 us
  starting transfers between devices: 0.61 us -> 43.4 us
  loops' own time: 28 us -> 0 us
    dot_general x56 -> x0, matrix products: 261 us -> none  [the longest x8 77.8 us: conv_back_step(): jnp.einsum('rgmt,rgot->gmo', patches, grad_chan, preferred_element_type=j...]
    pallas_call x0 -> x6, Pallas kernels: none -> 173 us  [call(): pl.pallas_call(kernel, out_shape=[jax.ShapeDtypeStruct(s, d) for s, d in...]
    psum x4 -> x0, waiting for transfers between devices: 151 us -> none  [the longest x1 51.5 us: local(): lax.psum(jnp.einsum('nf,df->nd', hidden_grad, up_back, preferred_element_...]
    while x360 -> x0, other arithmetic: 139 us -> none
    another operation x24 -> x6, local copies, waits for them, and re-layouts: 109 us -> 2.11 us  [the longest x1 1.07 us: local(): small_s[0].reshape(rows, 1)]
    reshape x11 -> x3, local copies, waits for them, and re-layouts: 101 us -> 2.06 us  [the longest x2 2.05 us: local(): seg_c, mask_c = (segment_ids.reshape(rows, 1), time_mask.reshape(rows, 1))]
    all_gather x4 -> x0, blocking collectives: 83.3 us -> none  [the longest x1 21.9 us: local(): lax.all_gather(value_weight, 'dp', axis=0, tiled=True)]
    unnamed x15 -> x5, waiting for transfers between devices: 1.93 us -> 76.8 us
  transfers between devices with their start and end apart: 15 -> 18, of which waited for: 7 -> 9; matrix products, arithmetic and copies ran while one was open for 35% -> 7% of each run, Pallas kernels for 0% -> 13%
where the time goes in v1:
time: 570 us; the launch traced here: 561 us
  waiting for transfers between devices  224 us (39%)
  Pallas kernels  173 us (30%)
  local copies, waits for them, and re-layouts  44.7 us (8%)
  starting transfers between devices  43.4 us (8%)
  blocking collectives  41.4 us (7%)
  other arithmetic  17.8 us (3%)
  between operations  16.6 us (3%)
    pallas_call x6, Pallas kernels, call(): pl.pallas_call(kernel, out_shape=[jax.ShapeDtypeStruct(s, d) for s, d in...  173 us
    unnamed x5, waiting for transfers between devices  76.8 us
    all_gather x1, waiting for transfers between devices, local(): lax.all_gather(turned(wall), BOTH, axis=0, tiled=True, axis_index_groups=...  48.5 us
    ppermute x1, waiting for transfers between devices, local(): other_out = lax.ppermute(out_s, 'mp', [(0, 1), (1, 0)])  43 us
    psum x1, blocking collectives, local(): flat = lax.psum(flat, BOTH)  41.4 us
    all_gather x1, waiting for transfers between devices, local(): conv_full = lax.all_gather(conv_weight.T, 'dp', axis=0, tiled=True)  40.8 us
    ppermute x8, starting transfers between devices, local(): swap = lambda v: lax.ppermute(v, BOTH, sibling)  16.9 us
    ppermute x1, starting transfers between devices, local(): other_out = lax.ppermute(out_s, 'mp', [(0, 1), (1, 0)])  14.9 us
  transfers between devices with their start and end apart: 18, of which 9 were waited for; matrix products, arithmetic and copies ran while one was open for 7% of the time, Pallas kernels for 13%

profile of v1, /device:TPU:0, one launch (start us, length us, event | category | flops | bytes accessed | tf_op | source)
XLA Modules:
  0.0 561.1 jit_solution(14038175758389863165)
XLA Ops:
  7.3 0.7 all-gather.3.cloned.1.call-update
  8.0 0.8 constant_dynamic-update-slice_fusion.3
  8.8 0.8 constant_dynamic-update-slice_fusion.2
  9.6 0.8 constant_dynamic-update-slice_fusion.1
  10.4 0.8 bitcast_dynamic-update-slice_fusion.1
  11.1 0.9 constant_dynamic-update-slice_fusion
  12.1 0.9 bitcast_dynamic-update-slice_fusion
  13.0 0.7 collective-permute-start.4
  13.7 0.8 copy-done.10
  14.5 10.7 %collective-permute-start = (bf16[1024,768]{1,0:T(8,128)(2,1)S(1)}, bf16[1024,768]{1,0:T(8,128)(2,1)S(1)}, u32[]{:S(2)}, u32[]{:S(2)}) collective-permute-start(bf16[1024,768]{1,0:T(8,128)(2,1)S(1)} %bitcast.42), channel_id=1, source_target_pairs={{0,2},{1,3},{2,0},{3,1},{4,6},{5,7},{6,4},{7,5},{8,10},{9,11},{10,... | collective-permute-start | bytes 4718600 | tf_op jit(solution)/shard_map/ppermute | solution.py:346
  25.3 1.0 copy.56.seg_ref
  27.0 1.2 fusion.1.x_ref
  28.2 40.8 %all-gather.3.cloned.1.call-done = bf16[6144,384]{0,1:T(8,128)(2,1)} async-done(((bf16[384,384]{0,1:T(8,128)(2,1)}), bf16[6144,384]{0,1:T(8,128)(2,1)}) %all-gather.3.cloned.1.call-update) | async-done | bytes 4718608 | tf_op jit(solution)/shard_map/all_gather | solution.py:351
  69.0 6.7 %copy.55 = bf16[6144,384]{1,0:T(8,128)(2,1)} copy(bf16[6144,384]{0,1:T(8,128)(2,1)} %all-gather.3.cloned.1.call-done) | data formatting | bytes 9437184 | tf_op jit(solution)/shard_map/all_gather | solution.py:351
  75.6 25.6 %shard_map.373 = (bf16[1024,384]{1,0:T(8,128)(2,1)}, f32[1024,384]{1,0:T(8,128)}) custom-call(s32[1024,1]{1,0:T(8,128)} %copy.56.seg_ref, bf16[1024,384]{1,0:T(8,128)(2,1)} %fusion.1.x_ref, bf16[16,384,384]{2,1,0:T(8,128)(2,1)} %bitcast.39, f32[1,384]{1,0:T(1,128)} %reshape.108.b_ref), custom_call_target="tpu_custom_call" | custom-call | tf_op jit(solution)/shard_map/pallas_call | solution.py:49
  101.2 7.5 %collective-permute-start.1 = (bf16[1024,384]{1,0:T(8,128)(2,1)}, bf16[1024,384]{1,0:T(8,128)(2,1)}, u32[]{:S(2)}, u32[]{:S(2)}) collective-permute-start(bf16[1024,384]{1,0:T(8,128)(2,1)} %get-tuple-element.53), channel_id=1, source_target_pairs={{0,0},{1,2},{2,1},{3,3},{4,4},{5,6},{6,5},{7,7},{8,8},{9,10},{10,9... | collective-permute-start | bytes 2359304 | tf_op jit(solution)/shard_map/ppermute | solution.py:347
  108.7 0.9 collective-permute-start.5
  110.9 5.1 collective-permute-start.2
  116.7 1.1 copy.58.segc_ref.seg_ref
  117.7 1.0 copy.57.mask_ref
  118.8 1.3 broadcast_select_fusion.1.hid_ref
  120.1 2.7 broadcast_select_fusion.2
  122.8 48.5 %all-gather.5.cloned.1.call-done = bf16[768,4608]{1,0:T(8,128)(2,1)} async-done(((bf16[48,4608]{1,0:T(8,128)(2,1)}), bf16[768,4608]{1,0:T(8,128)(2,1)}) %all-gather.5.cloned.1.call-update) | async-done | bytes 7077904 | tf_op jit(solution)/shard_map/all_gather | solution.py:357
  171.3 6.2 %fusion.9 = (bf16[768,1536]{1,0:T(8,128)(2,1)}, bf16[768,1536]{1,0:T(8,128)(2,1)}, bf16[768,1536]{1,0:T(8,128)(2,1)}) fusion(bf16[768,4608]{1,0:T(8,128)(2,1)} %all-gather.5.cloned.1.call-done), kind=kLoop, calls=%fused_computation.56 | loop fusion | bytes 14155776 | tf_op jit(solution)/shard_map/slice | solution.py:358
  177.5 26.0 %shard_map.374 = (f32[1024,768]{1,0:T(8,128)}, bf16[1024,768]{1,0:T(8,128)(2,1)}, bf16[1024,1152]{1,0:T(8,128)(2,1)}, bf16[1024,384]{1,0:T(8,128)(2,1)}, f32[6,1...) custom-call(bf16[1024,768]{1,0:T(8,128)(2,1)} %broadcast_select_fusion.1.hid_ref, ...), custom_call_target="tpu_custom_call" | custom-call | tf_op jit(solution)/shard_map/pallas_call | solution.py:49
  206.4 2.3 collective-permute-done.6.p1_ref
  208.7 1.1 copy-done.7
  209.8 18.1 %shard_map.375 = (f32[1024,768]{1,0:T(8,128)}, f32[1024,1]{1,0:T(8,128)}, bf16[1024,768]{1,0:T(8,128)(2,1)}, bf16[1024,1536]{1,0:T(8,128)(2,1)}, bf16[1024,1536]...) custom-call(f32[1024,768]{1,0:T(8,128)} %get-tuple-element.54.mixed_ref, ...), custom_call_target="tpu_custom_call" | custom-call | tf_op jit(solution)/shard_map/pallas_call | solution.py:49
  229.8 1.4 broadcast_select_fusion.cot_ref
  231.6 1.1 copy-done.5
  232.7 32.3 %shard_map.376 = (bf16[1024,768]{1,0:T(8,128)(2,1)}, f32[1024,768]{1,0:T(8,128)}, bf16[1024,768]{1,0:T(8,128)(2,1)}, bf16[768,1536]{1,0:T(8,128)(2,1)}, bf16[768...) custom-call(f32[1024,768]{1,0:T(8,128)} %get-tuple-element.56.n1_ref, f32[1,768]{1,0:T(1,128)} %reshape.111.g1_ref, ...), custom_call_target="tpu_custom_call" | custom-call | tf_op jit(solution)/shard_map/pallas_call | solution.py:49
  265.1 3.5 collective-permute-done.10.p1_ref
  268.6 1.1 copy-done.8
  269.8 39.2 %shard_map.377 = (f32[1024,384]{1,0:T(8,128)}, bf16[1024,384]{1,0:T(8,128)(2,1)}, bf16[768,1536]{1,0:T(8,128)(2,1)}, f32[3,768]{1,0:T(4,128)}, f32[1,1152]{1,0:T(1,128)}) custom-call(f32[1024,768]{1,0:T(8,128)} %get-tuple-element.63.gr2_ref, bf16[1024,768]{1,0:T(8,128)(2,1)} %get-tuple-element.64.p0_ref, bf16[1024,768]{1,0:T(8,128)(2,1)} %copy-done.8, ...), custom_call_target="tpu_custom_call" | custom-call | tf_op jit(solution)/shard_map/pallas_call | solution.py:49
  309.0 5.0 pad_maximum_fusion
  314.1 1.1 copy-done.32
  315.4 2.1 collective-permute-done.11
  317.7 0.7 collective-permute-start.12
  318.4 1.0 copy.63.mask_ref
  319.4 0.9 copy-done.9
  320.3 32.0 %shard_map.378 = (bf16[16,384,384]{2,1,0:T(8,128)(2,1)}, f32[1024,384]{1,0:T(8,128)}, f32[1,384]{1,0:T(1,128)}, f32[1,384]{1,0:T(1,128)}) custom-call(s32[1024,1]{1,0:T(8,128)} %copy.56.seg_ref, bf16[1024,384]{1,0:T(8,128)(2,1)} %fusion.1.x_ref, bf16[16,384,384]{2,1,0:T(8,128)(2,1)} %bitcast.40, f32[1024,384]{1,0:T(8,128)} %get-tuple-element.62.slope_ref, ...), custom_call_target="tpu_custom_call" | custom-call | tf_op jit(solution)/shard_map/pallas_call | solution.py:49
  352.5 1.3 copy-done.4
  353.8 14.9 %collective-permute-start.9 = (bf16[1024,768]{1,0:T(8,128)(2,1)S(1)}, bf16[1024,768]{1,0:T(8,128)(2,1)S(1)}, u32[]{:S(2)}, u32[]{:S(2)}) collective-permute-start(bf16[1024,768]{1,0:T(8,128)(2,1)S(1)} %copy-done.4), channel_id=1, source_target_pairs={{0,1},{1,0},{2,3},{3,2},{4,5},{5,4},{6,7},{7,6},{8,9},{9,8},{10,11... | collective-permute-start | bytes 4718600 | tf_op jit(solution)/shard_map/ppermute | solution.py:400
  368.7 0.6 fusion.5
  370.0 0.6 reduce_sum.45
  371.3 0.6 slice_reduce_fusion
  372.0 43.0 %collective-permute-done.9 = bf16[1024,768]{1,0:T(8,128)(2,1)S(1)} collective-permute-done((bf16[1024,768]{1,0:T(8,128)(2,1)S(1)}, bf16[1024,768]{1,0:T(8,128)(2,1)S(1)}, u32[]{:S(2)}, u32[]{:S(2)}) %collective-permute-start.9) | collective-permute-done | bytes 1572896 | tf_op jit(solution)/shard_map/ppermute | solution.py:400
  415.0 1.3 select_bitcast_fusion
  416.4 2.0 concatenate.26
  418.5 41.4 %psum.7 = f32[10757]{0:T(1024)S(1)} all-reduce(f32[10757]{0:T(1024)S(1)} %concatenate.26), channel_id=1, replica_groups=mesh['dp'=16,'mp'=2] {'dp','mp'}, use_global_device_ids=true, to_apply=%region_5.6 | all-reduce | flops 10757 | bytes 86056 | tf_op jit(solution)/shard_map/psum | solution.py:427
  460.5 0.6 fusion.11
  461.1 0.6 dynamic_slice.24
  461.8 0.6 dynamic_slice.25
  462.4 0.6 dynamic_slice.26
  463.1 0.6 dynamic_slice.23
  464.4 0.7 dynamic_slice.27
  465.0 6.5 %reduce-scatter.5.cloned.1.call-done = bf16[48,4608]{1,0:T(8,128)(2,1)} async-done(((bf16[768,4608]{1,0:T(8,128)(2,1)}), bf16[48,4608]{1,0:T(8,128)(2,1)}) %reduce-scatter.5.cloned.1.call-update) | async-done | bytes 442384 | tf_op jit(solution)/shard_map/reduce_scatter | solution.py:416
  471.6 1.7 collective-permute-start.13
  473.8 76.1 %reduce-scatter.7.cloned.1.call-done = bf16[384,384]{1,0:T(8,128)(2,1)} async-done(((bf16[6144,384]{1,0:T(8,128)(2,1)}), bf16[384,384]{1,0:T(8,128)(2,1)}) %reduce-scatter.7.cloned.1.call-update) | async-done | bytes 294928
  549.9 1.2 copy.66
  551.0 0.9 convert_bitcast_fusion
  552.0 0.7 slice_bitcast_fusion
  552.7 0.7 fusion.10
  553.4 0.7 split.28
  (123 shorter events, 9.8 us)
Async XLA Ops:
  7.2 7.3 %copy-start = (bf16[1,1024,768]{2,1,0:T(8,128)(2,1)S(1)}, bf16[1,1024,768]{2,1,0:T(8,128)(2,1)}, u32[]{:S(2)}) copy-start(bf16[1,1024,768]{2,1,0:T(8,128)(2,1)} %param.22) | copy-start | bytes 4718596
  7.2 18.1 %copy-start.11 = (s32[1,1024]{1,0:T(1,128)S(1)}, s32[1,1024]{1,0:T(1,128)}, u32[]{:S(2)}) copy-start(s32[1,1024]{1,0:T(1,128)} %param.24) | copy-start | bytes 12292
  7.2 18.1 %copy-start.12 = (s32[1,1024]{1,0:T(1,128)S(1)}, s32[1,1024]{1,0:T(1,128)}, u32[]{:S(2)}) copy-start(s32[1,1024]{1,0:T(1,128)} %param.23) | copy-start | bytes 12292
  7.2 19.1 %copy-start.31 = (bf16[384]{0:T(512)(128)(2,1)S(1)}, bf16[384]{0:T(512)(128)(2,1)}, u32[]{:S(2)}) copy-start(bf16[384]{0:T(512)(128)(2,1)} %param.27) | copy-start | bytes 2308
  7.2 19.7 %copy-start.16 = (bf16[768]{0:T(1024)(128)(2,1)S(1)}, bf16[768]{0:T(1024)(128)(2,1)}, u32[]{:S(2)}) copy-start(bf16[768]{0:T(1024)(128)(2,1)} %param.25) | copy-start | bytes 4612
  7.2 61.7 %all-gather.3.cloned.1.call-start = ((), (), s32[]{:S(2)}) async-start(), calls=%async_computation.2 | async-start | bytes 5013504 | tf_op jit(solution)/shard_map/all_gather | solution.py:351
  8.0 163.3 %all-gather.5.cloned.1.call-start = ((), (), s32[]{:S(2)}) async-start(), calls=%async_computation.3 | async-start | bytes 7520256 | tf_op jit(solution)/shard_map/all_gather | solution.py:357
  13.0 0.7 collective-permute-start.4
  13.7 0.8 copy-start.10
  14.5 457.1 %reduce-scatter.5.cloned.1.call-start = ((), (), s32[]{:S(2)}) async-start(), calls=%async_computation.4 | async-start | bytes 7520256 | tf_op jit(solution)/shard_map/reduce_scatter | solution.py:416
  14.5 104.2 %collective-permute-start = (bf16[1024,768]{1,0:T(8,128)(2,1)S(1)}, bf16[1024,768]{1,0:T(8,128)(2,1)S(1)}, u32[]{:S(2)}, u32[]{:S(2)}) collective-permute-start(bf16[1024,768]{1,0:T(8,128)(2,1)S(1)} %bitcast.42), channel_id=1, source_target_pairs={{0,2},{1,3},{2,0},{3,1},{4,6},{5,7},{6,4},{7,5},{8,10},{9,11},{10,... | collective-permute-start | bytes 4718600 | tf_op jit(solution)/shard_map/ppermute | solution.py:346
  75.6 33.0 %copy-start.17 = (bf16[1536]{0:T(1024)(128)(2,1)S(1)}, bf16[1536]{0:T(1024)(128)(2,1)}, u32[]{:S(2)}) copy-start(bf16[1536]{0:T(1024)(128)(2,1)} %param.38) | copy-start | bytes 9220
  75.6 33.0 %copy-start.29 = (bf16[384]{0:T(512)(128)(2,1)S(1)}, bf16[384]{0:T(512)(128)(2,1)}, u32[]{:S(2)}) copy-start(bf16[384]{0:T(512)(128)(2,1)} %param.32) | copy-start | bytes 2308
  75.6 33.0 %copy-start.30 = (bf16[384]{0:T(512)(128)(2,1)S(1)}, bf16[384]{0:T(512)(128)(2,1)}, u32[]{:S(2)}) copy-start(bf16[384]{0:T(512)(128)(2,1)} %param.31) | copy-start | bytes 2308
  101.2 9.7 %collective-permute-start.1 = (bf16[1024,384]{1,0:T(8,128)(2,1)}, bf16[1024,384]{1,0:T(8,128)(2,1)}, u32[]{:S(2)}, u32[]{:S(2)}) collective-permute-start(bf16[1024,384]{1,0:T(8,128)(2,1)} %get-tuple-element.53), channel_id=1, source_target_pairs={{0,0},{1,2},{2,1},{3,3},{4,4},{5,6},{6,5},{7,7},{8,8},{9,10},{10,9... | collective-permute-start | bytes 2359304 | tf_op jit(solution)/shard_map/ppermute | solution.py:347
  108.7 1.6 collective-permute-start.5
  109.7 6.4 %collective-permute-start.3 = (s32[2,1024]{1,0:T(2,128)S(1)}, s32[2,1024]{1,0:T(2,128)S(1)}, u32[]{:S(2)}, u32[]{:S(2)}) collective-permute-start(s32[2,1024]{1,0:T(2,128)S(1)} %pad_add_fusion), channel_id=1, source_target_pairs={{0,2},{1,3},{2,0},{3,1},{4,6},{5,7},{6,4},{7,5},{8,10},{9,11},{10,... | collective-permute-start | bytes 24584 | tf_op jit(solution)/shard_map/ppermute | solution.py:346
  110.9 9.2 %collective-permute-start.2 = (bf16[1024,384]{1,0:T(8,128)(2,1)}, bf16[1024,384]{1,0:T(8,128)(2,1)}, u32[]{:S(2)}, u32[]{:S(2)}) collective-permute-start(bf16[1024,384]{1,0:T(8,128)(2,1)} %collective-permute-done.1), channel_id=1, source_target_pairs={{0,2},{1,3},{2,0},{3,1},{4,6},{5,7},{6,4},{7,5},{8,10},{9,11},{10,... | collective-permute-start | bytes 2359304 | tf_op jit(solution)/shard_map/ppermute | solution.py:346
  177.5 26.0 %copy-start.3 = (bf16[1,1024,768]{2,1,0:T(8,128)(2,1)S(1)}, bf16[1,1024,768]{2,1,0:T(8,128)(2,1)}, u32[]{:S(2)}) copy-start(bf16[1,1024,768]{2,1,0:T(8,128)(2,1)} %param.43) | copy-start | bytes 4718596
  177.5 26.6 %copy-start.20 = (bf16[768]{0:T(1024)(128)(2,1)S(1)}, bf16[768]{0:T(1024)(128)(2,1)}, u32[]{:S(2)}) copy-start(bf16[768]{0:T(1024)(128)(2,1)} %param.35) | copy-start | bytes 4612
  177.5 27.1 %copy-start.21 = (bf16[768]{0:T(1024)(128)(2,1)S(1)}, bf16[768]{0:T(1024)(128)(2,1)}, u32[]{:S(2)}) copy-start(bf16[768]{0:T(1024)(128)(2,1)} %param.36) | copy-start | bytes 4612
  177.5 27.7 %copy-start.22 = (bf16[768]{0:T(1024)(128)(2,1)S(1)}, bf16[768]{0:T(1024)(128)(2,1)}, u32[]{:S(2)}) copy-start(bf16[768]{0:T(1024)(128)(2,1)} %param.34) | copy-start | bytes 4612
  203.6 5.1 collective-permute-start.6
  203.6 26.2 %collective-permute-start.8 = (bf16[1024,768]{1,0:T(8,128)(2,1)S(1)}, bf16[1024,768]{1,0:T(8,128)(2,1)S(1)}, u32[]{:S(2)}, u32[]{:S(2)}) collective-permute-start(bf16[1024,768]{1,0:T(8,128)(2,1)S(1)} %bitcast.43), channel_id=1, source_target_pairs={{0,2},{1,3},{2,0},{3,1},{4,6},{5,7},{6,4},{7,5},{8,10},{9,11},{10,... | collective-permute-start | bytes 4718600 | tf_op jit(solution)/shard_map/ppermute | solution.py:346
  208.7 1.1 copy-start.7
  209.8 18.2 %copy-start.23 = (bf16[768]{0:T(1024)(128)(2,1)S(1)}, bf16[768]{0:T(1024)(128)(2,1)}, u32[]{:S(2)}) copy-start(bf16[768]{0:T(1024)(128)(2,1)} %param.40) | copy-start | bytes 4612
  209.8 18.8 %copy-start.24 = (bf16[768]{0:T(1024)(128)(2,1)S(1)}, bf16[768]{0:T(1024)(128)(2,1)}, u32[]{:S(2)}) copy-start(bf16[768]{0:T(1024)(128)(2,1)} %param.41) | copy-start | bytes 4612
  209.8 19.4 %copy-start.25 = (bf16[768]{0:T(1024)(128)(2,1)S(1)}, bf16[768]{0:T(1024)(128)(2,1)}, u32[]{:S(2)}) copy-start(bf16[768]{0:T(1024)(128)(2,1)} %param.42) | copy-start | bytes 4612
  227.9 3.6 collective-permute-start.7
  231.5 1.1 copy-start.5
  265.0 3.6 collective-permute-start.10
  268.6 1.1 copy-start.8
  269.8 39.2 %copy-start.1 = (bf16[768,1536]{1,0:T(8,128)(2,1)S(1)}, bf16[768,1536]{1,0:T(8,128)(2,1)}, u32[]{:S(2)}) copy-start(bf16[768,1536]{1,0:T(8,128)(2,1)} %get-tuple-element.84) | copy-start | bytes 7077892
  269.8 39.2 %copy-start.2 = (bf16[768,1536]{1,0:T(8,128)(2,1)S(1)}, bf16[768,1536]{1,0:T(8,128)(2,1)}, u32[]{:S(2)}) copy-start(bf16[768,1536]{1,0:T(8,128)(2,1)} %get-tuple-element.83) | copy-start | bytes 7077892
  314.0 1.1 copy-start.32
  314.0 3.4 copy-start.6
  314.1 235.8 %reduce-scatter.7.cloned.1.call-start = ((), (), s32[]{:S(2)}) async-start(), calls=%async_computation.5 | async-start | bytes 5013504
  315.2 2.3 collective-permute-start.11
  317.7 1.7 collective-permute-start.12
  319.4 0.9 copy-start.9
  352.4 1.4 copy-start.4
  352.4 17.6 %copy-start.28 = (f32[1,384]{1,0:T(1,128)S(1)}, f32[1,384]{1,0:T(1,128)}, u32[]{:S(2)}) copy-start(f32[1,384]{1,0:T(1,128)} %get-tuple-element.80) | copy-start | bytes 4612
  352.4 18.9 %copy-start.15 = (f32[1,1536]{1,0:T(1,128)S(1)}, f32[1,1536]{1,0:T(1,128)}, u32[]{:S(2)}) copy-start(f32[1,1536]{1,0:T(1,128)} %get-tuple-element.76) | copy-start | bytes 18436
  352.4 18.9 %copy-start.13 = (f32[5,768]{1,0:T(8,128)S(1)}, f32[5,768]{1,0:T(8,128)}, u32[]{:S(2)}) copy-start(f32[5,768]{1,0:T(8,128)} %get-tuple-element.77) | copy-start | bytes 46084
  352.4 18.9 %copy-start.14 = (f32[3,768]{1,0:T(4,128)S(1)}, f32[3,768]{1,0:T(4,128)}, u32[]{:S(2)}) copy-start(f32[3,768]{1,0:T(4,128)} %get-tuple-element.78) | copy-start | bytes 27652
  352.4 18.9 %copy-start.18 = (f32[1,768]{1,0:T(1,128)S(1)}, f32[1,768]{1,0:T(1,128)}, u32[]{:S(2)}) copy-start(f32[1,768]{1,0:T(1,128)} %get-tuple-element.79) | copy-start | bytes 9220
  352.4 19.5 %copy-start.19 = (f32[1,1152]{1,0:T(1,128)S(1)}, f32[1,1152]{1,0:T(1,128)}, u32[]{:S(2)}) copy-start(f32[1,1152]{1,0:T(1,128)} %get-tuple-element.75) | copy-start | bytes 13828
  353.8 61.2 %collective-permute-start.9 = (bf16[1024,768]{1,0:T(8,128)(2,1)S(1)}, bf16[1024,768]{1,0:T(8,128)(2,1)S(1)}, u32[]{:S(2)}, u32[]{:S(2)}) collective-permute-start(bf16[1024,768]{1,0:T(8,128)(2,1)S(1)} %copy-done.4), channel_id=1, source_target_pairs={{0,1},{1,0},{2,3},{3,2},{4,5},{5,4},{6,7},{7,6},{8,9},{9,8},{10,11... | collective-permute-start | bytes 4718600 | tf_op jit(solution)/shard_map/ppermute | solution.py:400
  372.0 44.3 %copy-start.27 = (f32[1,384]{1,0:T(1,128)S(1)}, f32[1,384]{1,0:T(1,128)}, u32[]{:S(2)}) copy-start(f32[1,384]{1,0:T(1,128)} %get-tuple-element.73) | copy-start | bytes 4612
  372.0 44.3 %copy-start.26 = (f32[1,384]{1,0:T(1,128)S(1)}, f32[1,384]{1,0:T(1,128)}, u32[]{:S(2)}) copy-start(f32[1,384]{1,0:T(1,128)} %get-tuple-element.74) | copy-start | bytes 4612
  471.6 80.3 %collective-permute-start.13 = (bf16[48,4608]{1,0:T(8,128)(2,1)}, bf16[48,4608]{1,0:T(8,128)(2,1)S(1)}, u32[]{:S(2)}, u32[]{:S(2)}) collective-permute-start(bf16[48,4608]{1,0:T(8,128)(2,1)} %reduce-scatter.5.cloned.1.call-done), channel_id=1, source_target_pairs={{0,0},{1,2},{2,1},{3,3},{4,4},{5,6},{6,5},{7,7},{8,8},{9,10},{10,9... | collective-permute-start | bytes 1327112 | tf_op jit(solution)/shard_map/ppermute | solution.py:347
Sparse Core Ops, SparseCore 0:
  10.2 58.6 all-gather.2
  71.8 99.4 all-gather.4
  314.2 157.3 reduce-scatter.4
  475.3 74.5 reduce-scatter.6

commit v2 on v1

v2 whole, which is shorter than its diff:
```python
import functools

import jax
import jax.numpy as jnp
from jax import lax
from jax.experimental import pallas as pl
from jax.experimental.pallas import tpu as pltpu
from jax.sharding import PartitionSpec as P

HD = 64
KW = 128
CG = 48
TAPS = 8
EPS = 1e-05
F32 = jnp.float32
BF16 = jnp.bfloat16
NN = (((1,), (0,)), ((), ()))
NT = (((1,), (1,)), ((), ()))
TN = (((0,), (0,)), ((), ()))
BOTH = ("dp", "mp")


def dg(a, b, dims):
    return lax.dot_general(a, b, dims, preferred_element_type=F32)


def gelu_parts(v):
    t = 1.0 / (1.0 + (0.3275911 * 0.7071067811865476) * jnp.abs(v))
    e = jnp.exp(-0.5 * v * v)
    poly = t * (0.254829592 + t * (-0.284496736 + t * (1.421413741 + t * (-1.453152027 + t * 1.061405429))))
    tail = 0.5 * poly * e
    return jnp.where(v >= 0, 1.0 - tail, tail), e


def gelu_and_slope(v):
    phi, e = gelu_parts(v)
    return v * phi, phi + v * e * 0.3989422804014327


def call(kernel, outs, scratch, *args, hbm_in=(), hbm_out=(), sems=(), meeting=None):
    space = lambda here: pl.BlockSpec(memory_space=pl.ANY if here else pltpu.VMEM)
    return pl.pallas_call(
        kernel,
        out_shape=[jax.ShapeDtypeStruct(s, d) for s, d in outs],
        in_specs=[space(i in hbm_in) for i in range(len(args))],
        out_specs=[space(i in hbm_out) for i in range(len(outs))],
        scratch_shapes=[pltpu.VMEM(s, d) for s, d in scratch] + [pltpu.SemaphoreType.DMA(s) for s in sems],
        compiler_params=pltpu.CompilerParams(vmem_limit_bytes=60 * 2**20, has_side_effects=bool(sems), collective_id=meeting),
    )(*args)


def split_low(v):
    hi = v.astype(BF16)
    return hi, (v - hi.astype(F32)).astype(BF16)


def spread_matrix(seg, length, width):
    rank = jnp.where(seg == 0, 7, seg - 1)
    pos = lax.broadcasted_iota(jnp.int32, (length, 1), 0) + 64 * rank + 8
    hit = pos == lax.broadcasted_iota(jnp.int32, (length, width), 1)
    return hit.astype(F32).astype(BF16)


def rolled(x, left):
    width = x.shape[1]
    left = left % width
    return x if left == 0 else pltpu.roll(x, width - left, 1)


def tap_patches(xg):
    return jnp.concatenate([rolled(xg, r) for r in range(TAPS)], axis=0)


def nothing(*_):
    pass


def block_rows(w_ref, at):
    w = w_ref[(slice(None),) * (len(w_ref.shape) - 2) + (at, slice(None))]
    return w.reshape(-1, w.shape[-1])


def conv_fwd_kernel(seg_ref, x_ref, w_ref, b_ref, low_ref, slope_ref, spread, xq, y_ref, ot, ready=nothing, beside=nothing):
    length, width = spread.shape
    blocks = KW // TAPS
    spread[...] = spread_matrix(seg_ref[...], length, width)
    xq[...] = dg(x_ref[...], spread[...], TN).astype(BF16)
    ready()

    def body(g, carry):
        beside(g)
        at = pl.ds(pl.multiple_of(g * CG, 16), CG)
        y_ref[...] = dg(block_rows(w_ref, at), tap_patches(xq[at, :]), NN)
        acc = rolled(y_ref[0:CG, :], -64)
        for b in range(1, blocks):
            acc = acc + rolled(y_ref[b * CG:(b + 1) * CG, :], TAPS * b - 64)
        ot[at, :] = acc
        return carry

    lax.fori_loop(0, x_ref.shape[1] // CG, body, 0)
    hi, lo = split_low(ot[...])
    pre = dg(spread[...], hi, NT) + dg(spread[...], lo, NT) + b_ref[...]
    valid = (seg_ref[...] != 0).astype(F32)
    value, slope = gelu_and_slope(pre)
    low_ref[...] = (valid * value).astype(BF16)
    slope_ref[...] = valid * slope


def conv_bwd_kernel(seg_ref, xq, w_ref, slope_ref, gm_ref, mask_ref, dw_ref, in_ref, db_ref, dm_ref,
                    spread, dq, d_ref, gq, extra=0, beside=nothing, store=None):
    length, width = spread.shape
    blocks = KW // TAPS
    groups = xq.shape[0] // CG
    spread[...] = spread_matrix(seg_ref[...], length, width)
    dpre = (slope_ref[...] * gm_ref[...].astype(F32)).astype(BF16)
    db_ref[...] = jnp.sum(dpre.astype(F32), axis=0, keepdims=True)
    dq[...] = dg(dpre, spread[...], TN).astype(BF16)

    def group(g):
        at = pl.ds(pl.multiple_of(g * CG, 16), CG)
        dqg = dq[at, :]
        for b in range(blocks):
            d_ref[b * CG:(b + 1) * CG, :] = rolled(dqg, 64 - TAPS * b)
        dmat = d_ref[...]
        dw = dg(dmat, tap_patches(xq[at, :]), NT).astype(BF16).reshape(blocks, CG, TAPS * CG)
        if store is None:
            dw_ref[:, at, :] = dw
        else:
            store(g, dw)
        v = dg(block_rows(w_ref, at), dmat, TN)
        acc = v[0:CG, :]
        for r in range(1, TAPS):
            acc = acc + rolled(v[r * CG:(r + 1) * CG, :], -r)
        gq[at, :] = acc

    def body(g, carry):
        if extra:
            pl.when(g < groups)(lambda: group(g))
        else:
            group(g)
        beside(g)
        return carry

    lax.fori_loop(0, groups + extra, body, 0)
    hi, lo = split_low(gq[...])
    grad = dg(spread[...], hi, NT) + dg(spread[...], lo, NT) + gm_ref[...].astype(F32)
    masked = mask_ref[...].astype(F32)
    dm_ref[...] = jnp.sum(masked * grad, axis=0, keepdims=True)
    in_ref[...] = (1.0 - masked) * grad


class Place:
    def __init__(self):
        self.dp, self.y = lax.axis_index("dp"), lax.axis_index("mp")
        self.z, self.x, self.core = self.dp // 4, lax.rem(self.dp // 2, 2), lax.rem(self.dp, 2)

    def at(self, z=None, x=None, core=None, y=None):
        pick = lambda new, old: old if new is None else new
        dp = pick(z, self.z) * 4 + pick(x, self.x) * 2 + pick(core, self.core)
        return {"dp": dp, "mp": pick(y, self.y)}


def push(src, dst, sems, index, device):
    send, recv = sems if isinstance(sems, tuple) else (sems.at[0], sems.at[1])
    return pltpu.make_async_remote_copy(
        src_ref=src, dst_ref=dst, send_sem=send.at[index], recv_sem=recv.at[index],
        device_id=device, device_id_type=pl.DeviceIdType.MESH)


def meet(devices):
    here = pltpu.get_barrier_semaphore()
    for device in devices:
        pl.semaphore_signal(here, inc=1, device_id=device, device_id_type=pl.DeviceIdType.MESH)
    pl.semaphore_wait(here, len(devices))


def partners(p):
    return [p.at(z=lax.rem(p.z + o, 4)) for o in (1, 2, 3)] + [p.at(x=1 - p.x), p.at(core=1 - p.core), p.at(y=1 - p.y)]


def meet_all(p):
    crooked = p.core != p.y
    pl.when(crooked)(lambda: meet(partners(p) + [p.at(core=p.y, y=p.core)]))
    pl.when(jnp.logical_not(crooked))(lambda: meet(partners(p)))


class LineGather:
    UP, DOWN, ACROSS, LAST = range(4)

    def __init__(self, place, own, buf, send, recv, k, third, x_first=True):
        p = self.p = place
        self.own, self.buf, self.send, self.recv, self.k, self.x_first = own, buf, send, recv, k, x_first
        self.t = p.core if third == "core" else p.y
        over_x, over_t = p.at(x=1 - p.x), p.at(**{third: 1 - self.t})
        self.to = [p.at(z=jnp.minimum(p.z + 1, 3)), p.at(z=jnp.maximum(p.z - 1, 0))] + ([over_x, over_t] if x_first else [over_t, over_x])

    def slot(self, z, across=False, last=False):
        flip = lambda v, yes: 1 - v if yes else v
        x, t = (across, last) if self.x_first else (last, across)
        return (z, flip(self.p.x, x), flip(self.t, t))

    def copy(self, way, slot, src=None):
        at = (self.k,) + slot
        return pltpu.make_async_remote_copy(
            src_ref=self.buf.at[slot] if src is None else src, dst_ref=self.buf.at[slot], send_sem=self.send.at[(way,) + at],
            recv_sem=self.recv.at[at], device_id=self.to[way], device_id_type=pl.DeviceIdType.MESH)

    def walk(self, d, start, finish):
        p = self.p
        if d == 0:
            mine = self.slot(p.z)
            pl.when(p.z < 3)(lambda: start(self.UP, mine, True))
            pl.when(p.z > 0)(lambda: start(self.DOWN, mine, True))
            start(self.ACROSS, mine, True)
            start(self.LAST, mine, True)
            return

        def passing(z, way, further):
            slot = self.slot(z)
            finish(slot)
            pl.when(further)(lambda: start(way, slot, False))
            start(self.ACROSS, slot, False)
            start(self.LAST, slot, False)

        def crossed(z):
            slot = self.slot(z, across=True)
            finish(slot)
            start(self.LAST, slot, False)

        if d < 4:
            pl.when(p.z >= d)(lambda: passing(p.z - d, self.UP, p.z < 3))
            pl.when(p.z + d <= 3)(lambda: passing(p.z + d, self.DOWN, p.z > 0))
        if d == 1:
            crossed(p.z)
        else:
            pl.when(p.z >= d - 1)(lambda: crossed(p.z - d + 1))
            pl.when(p.z + d - 1 <= 3)(lambda: crossed(p.z + d - 1))

    def begin(self, way, slot, own):
        self.copy(way, slot, self.own if own else None).start()

    def round(self, d):
        self.walk(d, self.begin, lambda slot: self.copy(0, slot).wait_recv())

    def drain(self):
        for z in range(4):
            for across in (False, True):
                self.copy(0, self.slot(z, across, True)).wait_recv()
        for d in range(5):
            self.walk(d, lambda way, slot, own: self.copy(way, slot, self.own if own else None).wait_send(), nothing)


class Fold:
    def __init__(self, kind, place, grad, sems, k, first, across, out1, cur, mid, last, out):
        self.kind, self.p, self.d, self.first, self.across, self.out1 = kind, place, grad, first, across, out1
        self.cur, self.mid, self.last, self.out = cur, mid, last, out
        p = place
        self.straight = p.core == p.y
        copy = lambda src, dst, n, dev: push(src, dst, sems, (k, n), dev)
        home, partner, sibling = p.at(y=p.core), p.at(x=1 - p.x), p.at(core=1 - p.core)
        away = grad.at[:, 1 - p.x]
        if kind == 0:
            self.over_y = copy(grad, first, 0, home)
            self.to_sibling = copy(out1, cur, 1, sibling)
            self.over_x = copy(cur.at[:, 1 - p.x], across, 2, partner)
        else:
            self.over_x = copy(away, across, 2, partner)
            self.over_y = copy(mid, first, 0, home)
            self.to_sibling = copy(out1, cur, 1, sibling)
        held = mid if kind == 0 else cur
        self.along = [copy(held.at[lax.rem(p.z + o, 4)], last.at[o - 1], 2 + o, p.at(z=lax.rem(p.z + o, 4))) for o in (1, 2, 3)]
        self.held = held

    def one_way(self, copy, sends, wait):
        pl.when(sends)(copy.wait_send if wait else copy.start)
        if wait:
            pl.when(jnp.logical_not(sends))(copy.wait_recv)

    def start(self, n):
        p, wide = self.p, lambda ref: ref.astype(F32)
        crooked = jnp.logical_not(self.straight)
        if n == 0:
            if self.kind == 0:
                self.one_way(self.over_y, crooked, False)
            else:
                self.over_x.start()
        elif n == 1:
            if self.kind == 0:
                @pl.when(self.straight)
                def _():
                    for z in range(4):
                        for x in range(2):
                            self.cur[z, x] = (wide(self.d[z, x, p.core]) + wide(self.first[z, x, p.core])).astype(BF16)
                            self.out1[z, x] = (wide(self.d[z, x, 1 - p.core]) + wide(self.first[z, x, 1 - p.core])).astype(BF16)
                    self.to_sibling.start()
            else:
                for z in range(4):
                    for c in range(2):
                        self.mid[z, c] = (wide(self.d[z, p.x, c]) + wide(self.across[z, c])).astype(BF16)
                self.one_way(self.over_y, crooked, False)
        elif n == 2:
            if self.kind == 0:
                self.over_x.start()
            else:
                @pl.when(self.straight)
                def _():
                    for z in range(4):
                        self.cur[z] = (wide(self.mid[z, p.core]) + wide(self.first[z, p.core])).astype(BF16)
                        self.out1[z] = (wide(self.mid[z, 1 - p.core]) + wide(self.first[z, 1 - p.core])).astype(BF16)
                    self.to_sibling.start()
        elif n == 3:
            if self.kind == 0:
                for z in range(4):
                    self.mid[z] = (wide(self.cur[z, p.x]) + wide(self.across[z])).astype(BF16)
            for c in self.along:
                c.start()
        else:
            self.out[...] = wide(self.held[p.z]) + wide(self.last[0]) + wide(self.last[1]) + wide(self.last[2])

    def wait(self, n):
        crooked = jnp.logical_not(self.straight)
        if n == 3:
            for c in self.along:
                c.wait()
        elif (self.kind, n) in ((0, 0), (1, 1)):
            self.one_way(self.over_y, crooked, True)
        elif (self.kind, n) in ((0, 1), (1, 2)):
            self.one_way(self.to_sibling, self.straight, True)
        else:
            self.over_x.wait()


def fold_scratch(kind, n):
    wide = (4, 2, 48, n)
    if kind == 0:
        shapes = ((4, 2, 2, 48, n), (4, 48, n), wide, wide, (4, 48, n), (3, 48, n))
    else:
        shapes = (wide, wide, (4, 48, n), (4, 48, n), wide, (3, 48, n))
    return [(s, BF16) for s in shapes]


def columns(rows_ref):
    return rows_ref[...].astype(F32).T


def conv_gather_kernel(*refs):
    (small_ref, hid_ref, cot_ref, emb_ref, shard_ref, b_ref, qk, vo, ul, ur,
     xq, slope_ref, conv_t, hid_s, cot_s, small_s, w_out, wqk, wvo, wul, wur,
     spread, y_ref, ot, low, w_ref, own_t, seg, x_ref, local, turn, send_c, recv_c, send_w, recv_w) = refs
    p = Place()
    straight = p.core == p.y
    crooked = jnp.logical_not(straight)
    meet_all(p)
    shards = (qk, vo, ul, ur)
    walls = (wqk, wvo, wul, wur)
    conv = LineGather(p, shard_ref, w_ref, send_c, recv_c, 0, "core")
    gathers = [LineGather(p, own_t.at[k], walls[k], send_w, recv_w, k, "y", k < 3) for k in range(4)]
    own_w = pltpu.make_async_copy(shard_ref, w_ref.at[p.z, p.x, p.core], local.at[0])
    save_w = pltpu.make_async_copy(w_ref, w_out, local.at[1])
    keep = [pltpu.make_async_copy(own_t.at[k], walls[k].at[p.z, p.x, p.y], local.at[2 + k]) for k in range(4)]
    turned = [push(shards[k], own_t.at[k], turn, (k,), p.at(core=p.y, y=p.core)) for k in range(4)]
    pairs = ((hid_ref, hid_s), (cot_ref, cot_s), (small_ref, small_s))
    keep_rows = [pltpu.make_async_copy(a, b, local.at[6 + k]) for k, (a, b) in enumerate(pairs)]
    push_rows = [push(a, b, turn, (4 + k,), p.at(core=1 - p.core)) for k, (a, b) in enumerate(pairs)]
    turn_conv = push(low, conv_t, turn, (7,), p.at(core=p.y, y=p.core))

    own_w.start()
    conv.round(0)

    @pl.when(straight)
    def _():
        for k in range(4):
            own_t[k] = shards[k][...]
        for c in keep_rows + push_rows:
            c.start()

    @pl.when(crooked)
    def _():
        for c in turned:
            c.start()

    cols = columns(small_ref)
    seg[...] = cols[:, 0:1].astype(jnp.int32)
    mine = pl.ds(pl.multiple_of(p.y * x_ref.shape[1], 128), x_ref.shape[1])
    hid = hid_ref[:, mine].astype(F32)
    x_ref[...] = (hid + cols[:, 1:2] * (emb_ref[:, mine] - hid)).astype(BF16)

    def ready():
        for d in (1, 2, 3):
            conv.round(d)

        @pl.when(crooked)
        def _():
            for c in turned:
                c.wait()

        for g in gathers:
            g.round(0)
        for c in keep:
            c.start()
        conv.round(4)
        conv.drain()
        own_w.wait()
        save_w.start()

    def beside(g):
        for at, d in ((1, 1), (3, 2), (5, 3), (7, 4)):
            @pl.when(g == at)
            def _(d=d):
                for gather in gathers:
                    gather.round(d)

    conv_fwd_kernel(seg, x_ref, w_ref, b_ref, low, slope_ref, spread, xq, y_ref, ot, ready, beside)

    @pl.when(straight)
    def _():
        conv_t[...] = low[...]
        for c in keep_rows:
            c.wait()
        for c in push_rows:
            c.wait_send()

    @pl.when(crooked)
    def _():
        turn_conv.start()
        for c in push_rows:
            c.wait_recv()

    for g in gathers:
        g.drain()
    for c in keep:
        c.wait()
    save_w.wait()
    pl.when(crooked)(turn_conv.wait)


def attn_gather_kernel(*refs):
    (hid_ref, conv_t, small_ref, emb_ref, wqk_ref, wvo_ref, qb_ref, vb_ref, dl, dr,
     mixed_ref, mlow_ref, qkv_ref, ctx_ref, lse_ref, part_ref, other_ref, stat_ref, wdl, wdr,
     qt, vt, ot, both, own_t, segc, mask, local, turn, send_w, recv_w, send_p, recv_p) = refs
    p = Place()
    crooked = p.core != p.y
    sibling = p.at(core=1 - p.core)
    meet_all(p)
    shards, walls = (dl, dr), (wdl, wdr)
    gathers = [LineGather(p, own_t.at[k], walls[k], send_w, recv_w, k, "y", k == 0) for k in range(2)]
    keep = [pltpu.make_async_copy(own_t.at[k], walls[k].at[p.z, p.x, p.y], local.at[k]) for k in range(2)]
    turned = [push(shards[k], own_t.at[k], turn, (k,), p.at(core=p.y, y=p.core)) for k in range(2)]
    give = push(conv_t, both.at[p.core], turn, (2,), sibling)
    give.start()

    @pl.when(crooked)
    def _():
        for c in turned:
            c.start()

    @pl.when(jnp.logical_not(crooked))
    def _():
        for k in range(2):
            own_t[k] = shards[k][...]

    both[p.core] = conv_t[...]
    cols = columns(small_ref)
    segc[...] = cols[:, 0:1].astype(jnp.int32)
    mask[...] = cols[:, 1:2].astype(jnp.int32)

    @pl.when(crooked)
    def _():
        for c in turned:
            c.wait()

    for g in gathers:
        g.round(0)
    for c in keep:
        c.start()
    give.wait()

    def beside(n):
        for at, d in ((-1, 1), (0, 2), (1, 3), (2, 4)):
            if isinstance(n, int):
                if n == at:
                    for g in gathers:
                        g.round(d)
            elif at >= 0:
                @pl.when(n == at)
                def _(d=d):
                    for g in gathers:
                        g.round(d)

    def sent(i, at):
        c = push(part_ref.at[at], other_ref.at[at], (send_p, recv_p), (i,), sibling)
        c.start()
        return c

    copies = attn_fwd_kernel(hid_ref, both.at[0], both.at[1], mask, segc, small_ref.at[0:1], emb_ref, (wqk_ref, wvo_ref), qb_ref, vb_ref,
                             mixed_ref, mlow_ref, qkv_ref, ctx_ref, lse_ref, part_ref, stat_ref, qt, vt, ot, beside, sent)
    for g in gathers:
        g.drain()
    for c in keep + copies:
        c.wait()


def attn_fwd_kernel(hid_ref, c0_ref, c1_ref, mask_ref, segc_ref, segr_ref, emb_ref, w_refs, qb_ref, vb_ref,
                    mixed_ref, mlow_ref, qkv_ref, ctx_ref, lse_ref, part_ref, stat_ref, qt, vt, ot, beside=nothing, sent=nothing):
    wqk_ref, wvo_ref = w_refs
    rows, width = hid_ref.shape
    half = c0_ref.shape[1]
    heads = half // HD
    step = 256
    stat = jnp.zeros((1, half), F32)
    for i in range(rows // step):
        at = pl.ds(i * step, step)
        conv = jnp.concatenate([c0_ref[at, :].astype(F32), c1_ref[at, :].astype(F32)], axis=1)
        hid = hid_ref[at, :].astype(F32)
        masked = mask_ref[at, :].astype(F32)
        mixed = hid + masked * (emb_ref[...] - hid) + conv
        low = mixed.astype(BF16)
        mixed_ref[at, :] = mixed
        mlow_ref[at, :] = low
        stat = stat + jnp.sum(conv[:, :half] * conv[:, :half] + conv[:, half:] * conv[:, half:], axis=0, keepdims=True)
        qk = dg(low, wqk_ref[...], NN)
        qkv_ref[at, 0:half] = (qk[:, :half] + qb_ref[...]).astype(BF16)
        qkv_ref[at, half:2 * half] = qk[:, half:].astype(BF16)
        qkv_ref[at, 2 * half:] = (dg(low, wvo_ref[:, :half], NN) + vb_ref[...]).astype(BF16)
    stat_ref[...] = stat
    beside(-1)
    qt[...] = (qkv_ref[:, 0:half] * jnp.asarray(HD ** -0.5, BF16)).T
    vt[...] = qkv_ref[:, 2 * half:].T

    def pair_body(p, carry):
        beside(p)
        lanes = pl.ds(pl.multiple_of(half + p * 128, 128), 128)
        k_pair = qkv_ref[:, lanes]
        for j in range(2):
            head_at = pl.ds(pl.multiple_of(p * 128 + j * HD, HD), HD)
            qh = qt[head_at, :]
            vh = vt[head_at, :]
            zero = jnp.zeros_like(qh)
            qz = jnp.concatenate([qh, zero] if j == 0 else [zero, qh], axis=0)
            for i in range(rows // step):
                at = slice(i * step, (i + 1) * step)
                s = dg(k_pair, qz[:, at], NN)
                s = jnp.where(segc_ref[...] == segr_ref[:, at], s, -1000000000.0)
                top = jnp.max(s, axis=0, keepdims=True)
                e = jnp.exp(s - top)
                den = jnp.sum(e, axis=0, keepdims=True)
                o = dg(vh, e.astype(BF16), NN) / den
                ot[head_at, at] = jnp.where(segr_ref[:, at] != 0, o, 0.0).astype(BF16)
                lse_ref[pl.ds(2 * p + j, 1), at] = top + jnp.log(den)
        return carry

    lax.fori_loop(0, heads // 2, pair_body, 0)
    ctx_ref[...] = ot[...].T
    copies = []
    for i in range(rows // step):
        at = pl.ds(i * step, step)
        part_ref[at, :] = dg(ctx_ref[at, :], wvo_ref[:, half:], NT).astype(BF16)
        copies.append(sent(i, at))
    return copies


def norm_stats(x):
    centre = x - jnp.mean(x, axis=-1, keepdims=True)
    r = lax.rsqrt(jnp.mean(centre * centre, axis=-1, keepdims=True) + EPS)
    return centre * r, r


def ffn_fwd_kernel(mixed_ref, p0_ref, p1_ref, seg_ref, ob_ref, g1_ref, s1_ref, ul_ref, ur_ref, ub_ref, dl_ref, dr_ref,
                   n1_ref, r1_ref, low_ref, hid_ref, slope_ref, part_ref, stat_ref, sent=nothing):
    rows, width = mixed_ref.shape
    ff = ul_ref.shape[1]
    step = 256
    stat_ref[...] = jnp.zeros_like(stat_ref)

    def body(i, carry):
        at = pl.ds(pl.multiple_of(i * step, step), step)
        attn = ob_ref[...] + (p0_ref[at, :].astype(F32) + p1_ref[at, :].astype(F32))
        valid = (seg_ref[at, :] != 0).astype(F32)
        stat_ref[...] += jnp.sum(valid * attn * attn, axis=0, keepdims=True)
        n1, r1 = norm_stats(mixed_ref[at, :] + attn)
        n1_ref[at, :] = n1
        r1_ref[at, :] = r1
        low = (n1 * g1_ref[...] + s1_ref[...]).astype(BF16)
        low_ref[at, :] = low
        part = 0.0
        for k, (up, down) in enumerate(((ul_ref, dl_ref), (ur_ref, dr_ref))):
            cols = slice(k * ff, (k + 1) * ff)
            value, slope = gelu_and_slope(dg(low, up[...], NN) + ub_ref[:, cols])
            hidden = value.astype(BF16)
            hid_ref[at, cols] = hidden
            slope_ref[at, cols] = slope.astype(BF16)
            part = part + dg(hidden, down[...], NT)
        part_ref[at, :] = part.astype(BF16)
        sent(i, at)
        return carry

    lax.fori_loop(0, rows // step, body, 0)


class Give:
    def __init__(self, place, part, other, sems):
        self.make = lambda i, at: push(part.at[at], other.at[at], sems, (i,), place.at(core=1 - place.core))

    def __call__(self, i, at):
        self.make(i, at).start()

    def wait(self, parts, step):
        for i in range(parts):
            self.make(i, pl.ds(i * step, step)).wait()


def ffn_fwd_give_kernel(*refs):
    ins, outs, other, seg, sems = refs[:12], refs[12:19], refs[19], refs[20], refs[21]
    p = Place()
    meet([p.at(core=1 - p.core)])
    seg[...] = columns(ins[3])[:, 0:1].astype(jnp.int32)
    give = Give(p, outs[5], other, sems)
    ffn_fwd_kernel(*ins[:3], seg, *ins[4:], *outs, give)
    give.wait(4, 256)


def norm_back(gn, n, r):
    return r * (gn - jnp.mean(gn, axis=-1, keepdims=True) - n * jnp.mean(gn * n, axis=-1, keepdims=True))


def ffn_bwd_kernel(n1_ref, g1_ref, s1_ref, p0_ref, p1_ref, seg_ref, db_ref, g2_ref, s2_ref, cot_ref, low_ref,
                   hid_ref, slope_ref, ul_ref, ur_ref, dl_ref, dr_ref,
                   out_ref, gr2_ref, part_ref, ddl_ref, ddr_ref, dul_ref, dur_ref, sums_ref, dub_ref, fg, hg,
                   done=None, down_done=nothing, sent=nothing):
    rows, width = n1_ref.shape
    ff = ul_ref.shape[1]
    step = 256
    sums_ref[...] = jnp.zeros_like(sums_ref)
    dub_ref[...] = jnp.zeros_like(dub_ref)
    row_sum = lambda v: jnp.sum(v, axis=0, keepdims=True)
    store = lambda ref, v: ref.__setitem__(Ellipsis, v.astype(ref.dtype).reshape(ref.shape))

    def norm_body(i, carry):
        at = pl.ds(pl.multiple_of(i * step, step), step)
        ffn = db_ref[...] + (p0_ref[at, :].astype(F32) + p1_ref[at, :].astype(F32))
        valid = (seg_ref[at, :] != 0).astype(F32)
        n2, r2 = norm_stats(n1_ref[at, :] * g1_ref[...] + s1_ref[...] + ffn)
        final = valid * (n2 * g2_ref[...] + s2_ref[...])
        if done is None:
            out_ref[at, :] = final.astype(BF16)
        else:
            done(i, at, final.astype(BF16))
        gf = valid * cot_ref[at, :].astype(F32)
        gr2 = norm_back(gf * g2_ref[...], n2, r2)
        gr2_ref[at, :] = gr2
        ffn_grad = gr2.astype(BF16)
        fg[at, :] = ffn_grad
        sums_ref[...] += jnp.concatenate(
            [row_sum(valid * ffn * ffn), row_sum(final * final), row_sum(gf * n2), row_sum(gf), row_sum(ffn_grad.astype(F32))], axis=0)
        return carry

    lax.fori_loop(0, rows // step, norm_body, 0)
    store(ddl_ref, dg(fg[...], hid_ref[:, :ff], TN))
    store(ddr_ref, dg(fg[...], hid_ref[:, ff:], TN))
    down_done()

    def body(i, carry):
        at = pl.ds(pl.multiple_of(i * step, step), step)
        part = 0.0
        for k, (up, down) in enumerate(((ul_ref, dl_ref), (ur_ref, dr_ref))):
            cols = slice(k * ff, (k + 1) * ff)
            hidden_grad = (slope_ref[at, cols].astype(F32) * dg(fg[at, :], down[...], NN)).astype(BF16)
            hg[at, cols] = hidden_grad
            dub_ref[:, cols] += row_sum(hidden_grad.astype(F32))
            part = part + dg(hidden_grad, up[...], NT)
        part_ref[at, :] = part.astype(BF16)
        sent(i, at)
        return carry

    lax.fori_loop(0, rows // step, body, 0)
    store(dul_ref, dg(low_ref[...], hg[:, :ff], TN))
    store(dur_ref, dg(low_ref[...], hg[:, ff:], TN))


def ffn_bwd_fold_kernel(*refs):
    ins, outs, (other, first_l, across_r), (fg, hg, seg), (sem_p, sem_o, sem_f) = refs[:17], refs[17:26], refs[26:29], refs[29:32], refs[32:]
    p = Place()
    straight = p.core == p.y
    home = p.at(y=p.core)
    meet([p.at(core=1 - p.core), p.at(x=1 - p.x), p.at(y=1 - p.y)])
    seg[...] = columns(ins[5])[:, 0:1].astype(jnp.int32)
    give = Give(p, outs[2], other, sem_p)
    out_ref, ddl, ddr = outs[0], outs[3], outs[4]
    show = lambda i: push(out_ref.at[pl.ds(i * 256, 256)], out_ref.at[pl.ds(i * 256, 256)], sem_o, (i,), p.at(y=1 - p.y))
    over_y = push(ddl, first_l, sem_f, (0,), home)
    over_x = push(ddr.at[:, 1 - p.x], across_r, sem_f, (1,), p.at(x=1 - p.x))

    def done(i, at, value):
        @pl.when(straight)
        def _():
            out_ref[at, :] = value
            push(out_ref.at[at], out_ref.at[at], sem_o, (i,), p.at(y=1 - p.y)).start()

    def down_done():
        pl.when(jnp.logical_not(straight))(over_y.start)
        over_x.start()

    ffn_bwd_kernel(*ins[:5], seg, *ins[6:], *outs, fg, hg, done, down_done, give)
    give.wait(4, 256)
    over_x.wait()

    @pl.when(straight)
    def _():
        over_y.wait_recv()
        for i in range(4):
            show(i).wait_send()

    @pl.when(jnp.logical_not(straight))
    def _():
        over_y.wait_send()
        for i in range(4):
            show(i).wait_recv()


def attn_bwd_kernel(gr2_ref, p0_ref, p1_ref, n1_ref, r1_ref, g1_ref, segc_ref, segr_ref, ctx_ref, qkv_ref, lse_ref,
                    mlow_ref, wqk_ref, wvo_ref,
                    dqk_ref, dvo_ref, sums_ref, dqkvb_ref, gr1, cg, qt, kt, ct, dqt, dk, dv, gqkv, finish, beside=nothing):
    rows, width = gr2_ref.shape
    half = ctx_ref.shape[1]
    heads = half // HD
    step = 256
    core = lax.rem(lax.axis_index("dp"), 2)
    sums_ref[...] = jnp.zeros_like(sums_ref)
    row_sum = lambda v: jnp.sum(v, axis=0, keepdims=True)

    def norm_body(i, carry):
        at = pl.ds(pl.multiple_of(i * step, step), step)
        gn1 = gr2_ref[at, :] + (p0_ref[at, :].astype(F32) + p1_ref[at, :].astype(F32))
        n1 = n1_ref[at, :]
        g = norm_back(gn1 * g1_ref[...], n1, r1_ref[at, :])
        gr1[at, :] = g
        attn_grad = g.astype(BF16)
        sums_ref[...] += jnp.concatenate([row_sum(gn1 * n1), row_sum(gn1), row_sum(attn_grad.astype(F32))], axis=0)
        back = dg(attn_grad, wvo_ref[:, half:], NN)
        cg[at, :] = jnp.where(segc_ref[at, :] != 0, back, 0.0).astype(BF16)
        return carry

    lax.fori_loop(0, rows // step, norm_body, 0)
    store = lambda ref, cols, v: ref.__setitem__((Ellipsis, cols), v.astype(BF16).reshape(ref.shape[:-1] + (v.shape[-1],)))
    store(dvo_ref, slice(half, 2 * half), dg(gr1[...].astype(BF16), ctx_ref[...], TN))
    scale = jnp.asarray(HD ** -0.5, BF16)
    qt[...] = (qkv_ref[:, 0:half] * scale).T
    kt[...] = qkv_ref[:, half:2 * half].T
    ct[...] = cg[...].T
    lane = lax.broadcasted_iota(jnp.int32, (1, 128), 1)

    def pair_body(p, carry):
        beside(p)
        base = pl.multiple_of(p * 128, 128)
        k_at = pl.ds(pl.multiple_of(half + base, 128), 128)
        v_at = pl.ds(pl.multiple_of(2 * half + base, 128), 128)
        q_pair = qkv_ref[:, pl.ds(base, 128)] * scale
        o_pair = cg[:, pl.ds(base, 128)]
        dk[...] = jnp.zeros_like(dk)
        dv[...] = jnp.zeros_like(dv)
        for j in range(2):
            head_at = pl.ds(pl.multiple_of(base + j * HD, HD), HD)
            zero = jnp.zeros((HD, rows), BF16)
            put = lambda a: jnp.concatenate([a, zero] if j == 0 else [zero, a], axis=0)
            qz, cz, kh = put(qt[head_at, :]), put(ct[head_at, :]), kt[head_at, :]
            keep = (lane < HD) if j == 0 else (lane >= HD)
            for i in range(rows // step):
                at = slice(i * step, (i + 1) * step)
                s = dg(qkv_ref[:, k_at], qz[:, at], NN)
                pr = jnp.exp(s - lse_ref[pl.ds(2 * p + j, 1), at])
                pr = jnp.where(segc_ref[...] == segr_ref[:, at], pr, 0.0)
                gp = dg(qkv_ref[:, v_at], cz[:, at], NN)
                delta = jnp.sum(pr * gp, axis=0, keepdims=True)
                ds = (pr * (gp - delta)).astype(BF16)
                dv[...] += dg(pr.astype(BF16), jnp.where(keep, o_pair[at, :], jnp.zeros_like(o_pair[at, :])), NN)
                dk[...] += dg(ds, jnp.where(keep, q_pair[at, :], jnp.zeros_like(q_pair[at, :])), NN)
                dqt[head_at, at] = (dg(kh, ds, NN) * (HD ** -0.5)).astype(BF16)
        gqkv[:, k_at] = dk[...].astype(BF16)
        gqkv[:, v_at] = dv[...].astype(BF16)
        return carry

    lax.fori_loop(0, heads // 2, pair_body, 0)
    gqkv[:, 0:half] = dqt[...].T
    mine = pl.ds(pl.multiple_of(core * half, 128), half)
    other = pl.ds(pl.multiple_of((1 - core) * half, 128), half)
    to_mixed = lambda at: (dg(gqkv[:, :2 * half], wqk_ref[at, :], NT) + dg(gqkv[:, 2 * half:], wvo_ref[at, 0:half], NT))
    finish(lambda: to_mixed(other).astype(BF16), lambda: gr1[:, mine] + to_mixed(mine))
    dqkvb_ref[...] = row_sum(gqkv[...].astype(F32))
    dqk_ref[...] = dg(mlow_ref[...], gqkv[:, :2 * half], TN).astype(BF16).reshape(dqk_ref.shape)
    store(dvo_ref, slice(0, half), dg(mlow_ref[...], gqkv[:, 2 * half:], TN))


def attn_bwd_plain_kernel(*refs):
    ins, outs, scratch = refs[:14], refs[14:20], refs[20:]
    own_ref, send_ref = outs[:2]

    def finish(send, own):
        send_ref[...] = send()
        own_ref[...] = own()

    attn_bwd_kernel(*ins, *outs[2:], *scratch, finish)


def attn_bwd_fold_kernel(*refs):
    ins, (ddl, ddr, dul, dur, first_l, across_r) = refs[:13], refs[13:19]
    outs, (gm_out, out_dl, out_dr, out_ul, out_ur) = refs[19:23], refs[23:28]
    scratch, (segc, send, got, gm), bufs, (sem_f, sem_g) = refs[28:37], refs[37:41], refs[41:63], refs[63:]
    p = Place()
    straight = p.core == p.y
    meet_all(p)
    segc[...] = columns(ins[6])[:, 0:1].astype(jnp.int32)
    early = [Fold(0, p, ddl, sem_f, 0, first_l, *bufs[0:5], out_dl), Fold(1, p, ddr, sem_f, 1, bufs[5], across_r, *bufs[6:10], out_dr)]
    late = [Fold(0, p, dul, sem_f, 2, *bufs[10:16], out_ul), Fold(1, p, dur, sem_f, 3, *bufs[16:22], out_ur)]

    def step(folds, n, wait=True):
        for f in folds:
            if wait:
                f.wait(n - 1)
            f.start(n)

    step(late, 0, False)
    step(early, 1, False)

    def beside(pair):
        @pl.when(pair == 0)
        def _():
            step(early, 2)

        @pl.when(pair == 1)
        def _():
            step(early, 3)
            step(late, 1)

        @pl.when(pair == 2)
        def _():
            step(late, 2)
            step(early, 4)

    to_sibling = push(send, got, sem_g, (0,), p.at(core=1 - p.core))
    turn = push(gm, gm_out, sem_g, (1,), p.at(core=p.y, y=p.core))

    def finish(give, own):
        send[...] = give()
        to_sibling.start()
        step(late, 3)
        mine = own()
        to_sibling.wait()
        value = (mine + got[...].astype(F32)).astype(BF16)

        @pl.when(straight)
        def _():
            gm_out[...] = value

        @pl.when(jnp.logical_not(straight))
        def _():
            gm[...] = value
            turn.start()

    attn_bwd_kernel(*ins[:6], segc, ins[6].at[0:1], *ins[7:], *outs, *scratch, finish, beside)
    step(late, 4)
    pl.when(jnp.logical_not(straight))(turn.wait)


def share_and_add(vec, got, sems, p):
    hops = [p.at(core=1 - p.core), p.at(y=1 - p.y), p.at(x=1 - p.x)]
    for n, device in enumerate(hops):
        c = push(vec.at[n], got.at[n], sems, (n,), device)
        c.start()
        c.wait()
        vec[n + 1] = vec[n] + got[n]
    along = [push(vec.at[3], got.at[2 + o], sems, (2 + o,), p.at(z=lax.rem(p.z + o, 4))) for o in (1, 2, 3)]
    for c in along:
        c.start()
    for c in along:
        c.wait()
    return vec[3] + got[3] + got[4] + got[5]


def conv_fold_kernel(*refs):
    (small_ref, xq, w_ref, slope_ref, gm_ref, dqk, dvo, sums2, sums1, dqkvb, dub, stat_conv, stat_attn,
     in_ref, dconv_ref, out_qk, out_vo, vec_out, ub_out, rms_out, spread, dq, d_ref, gq) = refs[:24]
    seg_ref, mask_ref, db_ref, dm_ref, d_all, got_c, sum_c, got_x, sum_x, got_z, vec, got_v = refs[24:36]
    folds_bufs, (sem_c, sem_x, sem_z, sem_fold, sem_vec) = refs[36:48], refs[48:]
    p = Place()
    meet(partners(p))
    cols = columns(small_ref)
    seg_ref[...] = cols[:, 0:1].astype(jnp.int32)
    mask_ref[...] = cols[:, 1:2].astype(jnp.int32)
    groups = 8
    folds = [Fold(0, p, dqk, sem_fold, 0, *folds_bufs[:6], out_qk), Fold(0, p, dvo, sem_fold, 1, *folds_bufs[6:], out_vo)]
    for f in folds:
        f.start(0)

    def store(g, dw):
        d_all[g] = dw.reshape(d_all.shape[1:])

    to_c = lambda g: push(d_all.at[g, :, :, 1 - p.core], got_c.at[g], sem_c, (g,), p.at(core=1 - p.core))
    to_x = lambda g: push(sum_c.at[g, :, 1 - p.x], got_x.at[g], sem_x, (g,), p.at(x=1 - p.x))
    to_z = lambda g: [push(sum_x.at[g, lax.rem(p.z + o, 4)], got_z.at[g, o - 1], sem_z, (g, o - 1), p.at(z=lax.rem(p.z + o, 4)))
                      for o in (1, 2, 3)]
    wide = lambda v: v.astype(F32)

    def beside(g):
        @pl.when(g < groups)
        def _():
            to_c(g).start()

        @pl.when(jnp.logical_and(g >= 1, g <= groups))
        def _():
            k = g - 1
            to_c(k).wait()
            for z in range(4):
                for x in range(2):
                    sum_c[k, z, x] = (wide(d_all[k, z, x, p.core]) + wide(got_c[k, z, x])).astype(BF16)
            to_x(k).start()

        @pl.when(jnp.logical_and(g >= 2, g <= groups + 1))
        def _():
            k = g - 2
            to_x(k).wait()
            for z in range(4):
                sum_x[k, z] = (wide(sum_c[k, z, p.x]) + wide(got_x[k, z])).astype(BF16)
            for c in to_z(k):
                c.start()

        for n, turn in ((1, 3), (2, 4), (3, 6)):
            @pl.when(g == turn)
            def _(n=n):
                for f in folds:
                    f.wait(n - 1)
                for f in folds:
                    f.start(n)

    conv_bwd_kernel(seg_ref, xq, w_ref, slope_ref, gm_ref, mask_ref, None, in_ref, db_ref, dm_ref,
                    spread, dq, d_ref, gq, 2, beside, store)
    width = vec.shape[2]
    half = width // 2
    by_core = (lax.broadcasted_iota(jnp.int32, (1, width), 1) // half == p.core).astype(F32)
    by_y = (lax.broadcasted_iota(jnp.int32, (1, width), 1) // half == p.y).astype(F32)
    twice = lambda v: jnp.concatenate([v, v], axis=1)
    is_core = lambda c: (p.core == c).astype(F32)
    frames = jnp.sum(wide(seg_ref[...] != 0), axis=0, keepdims=True)
    rows = [twice(dm_ref[...]) * by_y, twice(db_ref[...]) * by_y, twice(dqkvb[:, :half]) * by_core, twice(dqkvb[:, 2 * half:]) * by_core,
            sums1[2:3] * by_core, sums1[0:1] * by_core, sums1[1:2] * by_core, sums2[4:5] * by_core, sums2[2:3] * by_core, sums2[3:4] * by_core,
            dub[:, :width] * is_core(0), dub[:, width:] * is_core(0), dub[:, :width] * is_core(1), dub[:, width:] * is_core(1),
            twice(stat_conv[...]) * by_core * 0.5, stat_attn[...] * by_core, sums2[0:1] * by_core, sums2[1:2] * by_core,
            jnp.broadcast_to(frames * 0.5, (1, width))]
    rows.append(jnp.zeros((24 - len(rows), width), F32))
    vec[0] = jnp.concatenate(rows, axis=0)
    total = share_and_add(vec, got_v, sem_vec, p)
    vec_out[...] = total[:16]
    ub_out[...] = jnp.where(p.y == 0, total[10:12], total[12:14])
    powers = jnp.sum(total[14:18], axis=1, keepdims=True)
    rms_out[...] = jnp.broadcast_to(jnp.sqrt(powers / (total[18:19, 0:1] * width)), (4, 128))
    for f in folds:
        f.wait(3)
        f.start(4)
    for k in range(groups):
        for c in to_z(k):
            c.wait()
        piece = wide(sum_x[k, p.z]) + wide(got_z[k, 0]) + wide(got_z[k, 1]) + wide(got_z[k, 2])
        dq_at = slice(k * CG, (k + 1) * CG)
        gq[dq_at, 0:TAPS * CG] = piece
    dconv_ref[...] = gq[:, 0:TAPS * CG].T


def one_row(v):
    return v.astype(F32)[None]


def flat_turn(n_all):
    return [(f, f // 4 * 4 + (f % 2) * 2 + (f // 2) % 2) for f in range(n_all)]


def shapes(rows, width, ff):
    half = width // 2
    heads = half // HD
    spread_width = -(-(rows + 7 * 64 + 64) // 128) * 128
    blocks = KW // TAPS
    low, wide = lambda *s: (s, BF16), lambda *s: (s, F32)
    return dict(
        half=half, spread_width=spread_width, blocks=blocks,
        attn_out=[wide(rows, width), low(rows, width), low(rows, 3 * half), low(rows, half), wide(heads, rows), low(rows, width)],
        attn_scratch=[low(half, rows)] * 3,
        ffn_out=[wide(rows, width), wide(rows, 1), low(rows, width), low(rows, ff), low(rows, ff), low(rows, width), wide(1, width)],
        back_scratch=[wide(rows, width), low(rows, half), low(half, rows), low(half, rows), low(half, rows), low(half, rows),
                      wide(rows, 128), wide(rows, 128), low(rows, 3 * half)],
    )


def local_close(hidden_in, segment_ids, time_mask, mask_embed, conv_weight, conv_bias, query_weight, key_weight,
                value_weight, query_bias, value_bias, out_weight, out_bias, first_gain, first_shift, up_weight, up_bias,
                down_weight, down_bias, second_gain, second_shift, cotangent):
    _, rows, width = hidden_in.shape
    ff = up_weight.shape[1]
    n = ff // 2
    sh = shapes(rows, width, ff)
    half, sw, blocks = sh["half"], sh["spread_width"], sh["blocks"]
    low, wide = lambda *s: (s, BF16), lambda *s: (s, F32)
    down_t = down_weight.T
    shards = [jnp.concatenate([query_weight, key_weight], axis=1), jnp.concatenate([value_weight, out_weight.T], axis=1),
              up_weight[:, :n], up_weight[:, n:], down_t[:, :n], down_t[:, n:]]
    bias = lax.ppermute(jnp.concatenate([query_bias, value_bias, up_bias])[None], BOTH, flat_turn(32)).astype(F32)
    qb, vb, ub = bias[:, :half], bias[:, half:2 * half], bias[:, 2 * half:]
    small = jnp.concatenate([segment_ids, time_mask, jnp.zeros((6, rows), jnp.int32)], axis=0)
    emb, g1, s1 = one_row(mask_embed), one_row(first_gain), one_row(first_shift)
    seats = (4, 2, 2)
    wall = [low(*seats, 48, n)]

    xq, slope, conv_t, hid_s, cot_s, small_s, conv_full, w_qk, w_vo, w_ul, w_ur = call(
        conv_gather_kernel,
        [low(half, sw), wide(rows, half), low(rows, half), low(rows, width), low(rows, width), ((8, rows), jnp.int32),
         low(*seats, half, TAPS * CG)] + wall * 4,
        [low(rows, sw), wide(blocks * CG, sw), wide(half, sw), low(rows, half), low(*seats, half, TAPS * CG), low(4, 48, n),
         ((rows, 1), jnp.int32), low(rows, half)],
        small, hidden_in[0], cotangent[0], emb, conv_weight.T, one_row(conv_bias), *shards[:4],
        hbm_in=(4,), hbm_out=(3, 4, 5, 6, 7, 8, 9, 10),
        sems=((9,), (2, 8), (4, 1) + seats, (1,) + seats, (4, 4) + seats, (4,) + seats), meeting=1)
    flat = lambda w: w.reshape(width, n)
    w_qk, w_vo, w_ul, w_ur = flat(w_qk), flat(w_vo), flat(w_ul), flat(w_ur)
    mixed, mlow, qkv, ctx, lse, part1, other1, stat_conv, w_dl, w_dr = call(
        attn_gather_kernel, sh["attn_out"] + [low(rows, width), wide(1, half)] + wall * 2,
        sh["attn_scratch"] + [low(2, rows, half), low(2, 48, n), ((rows, 1), jnp.int32), ((rows, 1), jnp.int32)],
        hid_s, conv_t, small_s, emb, w_qk, w_vo, qb, vb, *shards[4:],
        hbm_out=(8, 9), sems=((2,), (2, 3), (4, 2) + seats, (2,) + seats, (4,), (4,)), meeting=2)
    w_dl, w_dr = flat(w_dl), flat(w_dr)
    n1, r1, nlow, hidden, hslope, part2, stat_attn, other2 = call(
        ffn_fwd_give_kernel, sh["ffn_out"] + [low(rows, width)], [((rows, 1), jnp.int32)],
        mixed, part1, other1, small_s, one_row(out_bias), g1, s1, w_ul, w_ur, ub, w_dl, w_dr, sems=((2, 4),), meeting=3)
    grad = low(*seats, 48, n)
    layer_out, gr2, part3, ddl, ddr, dul, dur, sums2, d_ub, other3, first_l, across_r = call(
        ffn_bwd_fold_kernel,
        [low(rows, width), wide(rows, width), low(rows, width)] + [grad] * 4 + [wide(5, width), wide(1, ff), low(rows, width), grad, low(4, 2, 48, n)],
        [low(rows, width), low(rows, ff), ((rows, 1), jnp.int32)],
        n1, g1, s1, part2, other2, small_s, one_row(down_bias), one_row(second_gain), one_row(second_shift), cot_s, nlow,
        hidden, hslope, w_ul, w_ur, w_dl, w_dr, sems=((2, 4), (2, 4), (2, 2)), meeting=4)
    own = [wide(48, n)]
    kinds = [fold_scratch(0, n)[1:], fold_scratch(1, n)[:1] + fold_scratch(1, n)[2:], fold_scratch(0, n), fold_scratch(1, n)]
    dqk, dvo, sums1, d_qkvb, gm, o_dl, o_dr, o_ul, o_ur = call(
        attn_bwd_fold_kernel,
        [grad, grad, wide(3, width), wide(1, 3 * half), low(rows, half)] + own * 4,
        sh["back_scratch"] + [((rows, 1), jnp.int32), low(rows, half), low(rows, half), low(rows, half)] + sum(kinds, []),
        gr2, part3, other3, n1, r1, g1, small_s, ctx, qkv, lse, mlow, w_qk, w_vo, ddl, ddr, dul, dur, first_l, across_r,
        sems=((2, 4, 6), (2, 2)), meeting=5)
    input_grad, d_conv, o_qk, o_vo, vec, d_ub, rms = call(
        conv_fold_kernel,
        [wide(rows, half), wide(TAPS * CG, half)] + own * 2 + [wide(16, width), wide(2, width), wide(4, 128)],
        [low(rows, sw), low(half, sw), low(blocks * CG, sw), wide(half, sw), ((rows, 1), jnp.int32), ((rows, 1), jnp.int32), wide(1, half), wide(1, half),
         low(8, *seats, CG, TAPS * CG), low(8, 4, 2, CG, TAPS * CG), low(8, 4, 2, CG, TAPS * CG), low(8, 4, CG, TAPS * CG),
         low(8, 4, CG, TAPS * CG), low(8, 3, CG, TAPS * CG), wide(4, 24, width), wide(6, 24, width)] + fold_scratch(0, n) * 2,
        small, xq, conv_full, slope, gm, dqk, dvo, sums2, sums1, d_qkvb, d_ub, stat_conv, stat_attn,
        sems=((2, 8), (2, 8), (2, 8, 3), (2, 2, 6), (2, 6)), meeting=6)
    y = lax.axis_index("mp")
    mine = lambda r: lax.dynamic_slice_in_dim(vec[r], y * half, half, 0)
    return (layer_out[None], input_grad[None], mine(0), d_conv, mine(1), o_qk[:, :half], o_qk[:, half:], o_vo[:, :half], mine(2), mine(3),
            o_vo[:, half:].T, vec[4], vec[5], vec[6], jnp.concatenate([o_ul, o_ur], axis=1), d_ub.reshape(ff),
            jnp.concatenate([o_dl, o_dr], axis=1).T, vec[7], vec[8], vec[9], rms[:, 0])


def local_any(n_dp, hidden_in, segment_ids, time_mask, mask_embed, conv_weight, conv_bias, query_weight, key_weight,
          value_weight, query_bias, value_bias, out_weight, out_bias, first_gain, first_shift, up_weight, up_bias,
          down_weight, down_bias, second_gain, second_shift, cotangent):
    _, rows, width = hidden_in.shape
    ff = up_weight.shape[1]
    n = ff // 2
    sh = shapes(rows, width, ff)
    half, spread_width, blocks = sh["half"], sh["spread_width"], sh["blocks"]
    part = lax.axis_index("mp")
    core = lax.rem(lax.axis_index("dp"), 2)
    n_all = 2 * n_dp
    turn = flat_turn(n_all)
    sibling = [(f, f ^ 2) for f in range(n_all)]
    core_groups = [[f for f in range(n_all) if (f // 2) % 2 == c] for c in range(2)]
    swap = lambda v: lax.ppermute(v, BOTH, sibling)
    turned = lambda v: lax.ppermute(v, BOTH, turn)
    mine = part == core

    down_t = down_weight.T
    w_shards = [jnp.concatenate([query_weight, key_weight], axis=1), jnp.concatenate([value_weight, out_weight.T], axis=1),
                up_weight[:, :n], up_weight[:, n:], down_t[:, :n], down_t[:, n:]]
    conv_full = lax.all_gather(conv_weight, "dp", axis=0, tiled=True)
    conv_full = conv_full.reshape(blocks, TAPS * CG, half).swapaxes(1, 2)
    w_qk, w_vo, w_ul, w_ur, w_dl, w_dr = (
        lax.all_gather(turned(w), BOTH, axis=0, tiled=True, axis_index_groups=core_groups) for w in w_shards)
    bias = turned(jnp.concatenate([query_bias, value_bias, up_bias])[None])
    qb, vb, ub = (b.astype(F32) for b in (bias[:, :half], bias[:, half:2 * half], bias[:, 2 * half:]))
    row = one_row

    hid, cot = hidden_in[0], cotangent[0]
    small = jnp.concatenate([segment_ids, time_mask], axis=0)
    hid_s = jnp.where(mine, hid, swap(hid))
    cot_s = jnp.where(mine, cot, swap(cot))
    small_s = jnp.where(mine, small, swap(small))
    seg_c, mask_c = segment_ids.reshape(rows, 1), time_mask.reshape(rows, 1)
    seg_sr, seg_sc, mask_sc = small_s[0:1], small_s[0].reshape(rows, 1), small_s[1].reshape(rows, 1)

    masked = mask_c.astype(F32)
    hid_half = lax.dynamic_slice_in_dim(hid, part * half, half, 1).astype(F32)
    emb_half = lax.dynamic_slice_in_dim(mask_embed, part * half, half, 0).astype(F32)
    start_half = (hid_half + masked * (emb_half - hid_half)).astype(BF16)
    low, wide = lambda *s: (s, BF16), lambda *s: (s, F32)
    def conv_kernel(seg_ref, x_ref, w_ref, b_ref, low_ref, slope_ref, xq, spread, y_ref, ot):
        conv_fwd_kernel(seg_ref, x_ref, w_ref, b_ref, low_ref, slope_ref, spread, xq, y_ref, ot)

    conv_low, conv_slope, xq = call(
        conv_kernel, [low(rows, half), wide(rows, half), low(half, spread_width)],
        [low(rows, spread_width), wide(blocks * CG, spread_width), wide(half, spread_width)],
        seg_c, start_half, conv_full, row(conv_bias))
    conv_s = turned(conv_low)
    conv_o = swap(conv_s)
    c0, c1 = jnp.where(core == 0, conv_s, conv_o), jnp.where(core == 0, conv_o, conv_s)

    def attn_kernel(*refs):
        attn_fwd_kernel(*refs[:7], refs[7:9], *refs[9:])

    mixed, mlow, qkv, ctx, lse, part1, stat_conv = call(
        attn_kernel, sh["attn_out"] + [wide(1, half)], sh["attn_scratch"],
        hid_s, c0, c1, mask_sc, seg_sc, seg_sr, row(mask_embed), w_qk, w_vo, qb, vb)
    n1, r1, nlow, hidden, slope, part2, stat_attn = call(
        ffn_fwd_kernel, sh["ffn_out"], [],
        mixed, part1, swap(part1), seg_sc, row(out_bias), row(first_gain), row(first_shift), w_ul, w_ur, ub, w_dl, w_dr)
    out_s, gr2, part3, ddl, ddr, dul, dur, sums2, d_ub = call(
        ffn_bwd_kernel,
        [low(rows, width), wide(rows, width), low(rows, width)] + [low(width, n)] * 4 + [wide(5, width), wide(1, ff)],
        [low(rows, width), low(rows, ff)],
        n1, row(first_gain), row(first_shift), part2, swap(part2), seg_sc, row(down_bias), row(second_gain), row(second_shift), cot_s, nlow,
        hidden, slope, w_ul, w_ur, w_dl, w_dr)
    other_out = lax.ppermute(out_s, "mp", [(0, 1), (1, 0)])
    layer_out = jnp.where(mine, out_s, other_out)[None]
    own, send, dqk, dvo, sums1, d_qkvb = call(
        attn_bwd_plain_kernel,
        [wide(rows, half), low(rows, half), low(width, 2 * half), low(width, 2 * half), wide(3, width), wide(1, 3 * half)], sh["back_scratch"],
        gr2, part3, swap(part3), n1, r1, row(first_gain), seg_sc, seg_sr, ctx, qkv, lse, mlow, w_qk, w_vo)
    gm_half = turned((own + swap(send).astype(F32)).astype(BF16))
    d_conv, input_grad, d_cb, d_me = call(
        conv_bwd_kernel,
        [low(blocks, half, TAPS * CG), wide(rows, half), wide(1, half), wide(1, half)],
        [low(rows, spread_width), low(half, spread_width), low(blocks * CG, spread_width), wide(half, spread_width)],
        seg_c, xq, conv_full, conv_slope, gm_half, mask_c)

    d_wall = jnp.concatenate([dqk, dvo, dul, dur, ddl, ddr], axis=1)
    d_wall = turned(lax.psum_scatter(d_wall, BOTH, scatter_dimension=0, tiled=True, axis_index_groups=core_groups)).astype(F32)
    d_conv = lax.psum_scatter(d_conv.swapaxes(1, 2).reshape(blocks * TAPS * CG, half), "dp", scatter_dimension=0, tiled=True).astype(F32)
    once = (jnp.arange(width) // half == core).astype(F32)[None]
    put = lambda v, which: lax.dynamic_update_slice(jnp.zeros((1, 2 * v.shape[1]), F32), v, (0, which * v.shape[1]))
    full = jnp.concatenate([sums2, sums1, stat_attn], axis=0) * once
    pieces = [put(d_me, part), put(d_cb, part), put(d_qkvb[:, :half], core), put(d_qkvb[:, 2 * half:], core), put(d_ub, core)]
    stats = jnp.stack([jnp.sum(stat_conv) * 0.5, jnp.sum(full[8]), jnp.sum(full[0]), jnp.sum(full[1]), jnp.sum((seg_c != 0).astype(F32)) * 0.5])
    flat = jnp.concatenate([jnp.concatenate(pieces, axis=1)[0], full[2:8].reshape(-1), stats])
    flat = lax.psum(flat, BOTH)
    at = 0
    sections = []
    for size in (width, width, width, width, 2 * ff) + (width,) * 6 + (5,):
        sections.append(flat[at:at + size])
        at += size
    me, cb, dqb, dvb, dub, g2, s2, db, g1, s1, ob, st = sections
    half_of = lambda v: lax.dynamic_slice_in_dim(v, part * (v.shape[0] // 2), v.shape[0] // 2, 0)
    stream_rms = jnp.sqrt(st[:4] / (st[4] * width))
    q_, k_, v_, o_, u_, d_ = jnp.split(d_wall, [half, 2 * half, 3 * half, 4 * half, 4 * half + ff], axis=1)
    return (layer_out, input_grad[None], half_of(me), d_conv, half_of(cb), q_, k_, v_, half_of(dqb), half_of(dvb), o_.T, ob, g1, s1,
            u_, half_of(dub), d_.T, db, g2, s2, stream_rms)


def solution(mesh):
    split, half, turn = P("dp", "mp"), P("mp"), P("mp", "dp")
    whole = P()
    rows = P("dp", None, None)
    return jax.shard_map(
        local_close if mesh.shape["dp"] == 16 else functools.partial(local_any, mesh.shape["dp"]),
        mesh=mesh,
        in_specs=(rows, P("dp", None), P("dp", None), whole, split, half, split, split, split, half, half, turn, whole, whole, whole,
                  split, half, turn, whole, whole, whole, rows),
        out_specs=(rows, P("dp", None, "mp"), half, split, half, split, split, split, half, half, turn, whole, whole, whole,
                   split, half, turn, whole, whole, whole, whole),
        check_vma=False,
    )
```

time: 570 us -> 433 us (0.76)
  waiting for transfers between devices: 224 us -> 0.01 us
  Pallas kernels: 173 us -> 389 us
  starting transfers between devices: 43.4 us -> 0.66 us
  blocking collectives: 41.4 us -> 0 us
  local copies, waits for them, and re-layouts: 44.7 us -> 28.8 us
  between operations: 16.6 us -> 1.25 us
  other arithmetic: 17.8 us -> 5.1 us
    pallas_call x6, Pallas kernels: 173 us -> 389 us  [call(): pl.pallas_call(kernel, out_shape=[jax.ShapeDtypeStruct(s, d) for s, d in...]
    all_gather x2 -> x0, waiting for transfers between devices: 89.3 us -> none  [the longest x1 48.5 us: local(): lax.all_gather(turned(wall), BOTH, axis=0, tiled=True, axis_index_groups=...]
    unnamed x5 -> x0, waiting for transfers between devices: 76.8 us -> none
    ppermute x14 -> x1, waiting for transfers between devices: 51.2 us -> 0.01 us  [local_close(): lax.ppermute(jnp.concatenate([query_bias, value_bias, up_bias])[None], BO...]
    ppermute x14 -> x1, starting transfers between devices: 43.2 us -> 0.66 us  [local_close(): lax.ppermute(jnp.concatenate([query_bias, value_bias, up_bias])[None], BO...]
    psum x1 -> x0, blocking collectives: 41.4 us -> none  [local(): flat = lax.psum(flat, BOTH)]
    unnamed x76 -> x24, local copies, waits for them, and re-layouts: 12.8 us -> 6.13 us
    all_gather x1 -> x0, local copies, waits for them, and re-layouts: 6.65 us -> none  [local(): conv_full = lax.all_gather(conv_weight.T, 'dp', axis=0, tiled=True)]
  transfers between devices with their start and end apart: 18 -> 1, of which waited for: 9 -> 0; matrix products, arithmetic and copies ran while one was open for 7% -> 4% of each run, Pallas kernels for 13% -> 22%
where the time goes in v2:
time: 433 us; the launch traced here: 425 us
  Pallas kernels  389 us (90%)
  local copies, waits for them, and re-layouts  28.8 us (7%)
  other arithmetic  5.1 us (1%)
    pallas_call x6, Pallas kernels, call(): pl.pallas_call(kernel, out_shape=[jax.ShapeDtypeStruct(s, d) for s, d in...  389 us
  transfers between devices with their start and end apart: 1, of which 0 were waited for; matrix products, arithmetic and copies ran while one was open for 4% of the time, Pallas kernels for 22%

profile of v2, /device:TPU:0, one launch (start us, length us, event | category | flops | bytes accessed | tf_op | source)
XLA Modules:
  0.0 424.9 jit_solution(5709310792841088273)
XLA Ops:
  0.7 0.0 copy-start.7
  0.7 0.0 copy-start.8
  0.7 0.0 copy-start.9
  0.7 0.7 pad_maximum_fusion.3
  1.4 0.7 collective-permute-start
  2.1 1.6 fusion.2
  3.7 0.1 pad.13.clone
  3.8 1.6 fusion.1
  5.4 1.4 add_add_fusion.refs_0_
  6.8 1.5 pad_maximum_fusion.1
  8.2 1.3 reshape.74.refs_3_
  9.5 1.8 copy.44
  11.4 1.2 reshape.75.refs_5_
  12.6 1.3 reshape.77.refs_5_.refs_1_
  13.9 1.3 reshape.78.refs_6_.refs_2_
  15.1 1.3 reshape.76.refs_4_
  16.4 0.0 copy-done.7
  16.4 0.6 reshape.79.refs_6_
  17.0 0.0 copy-done.8
  17.0 0.6 reshape.80.refs_7_
  17.6 0.0 copy-done.9
  17.6 0.6 reshape.81.refs_8_
  18.1 93.4 %shard_map.373 = (bf16[384,1536]{1,0:T(8,128)(2,1)}, f32[1024,384]{1,0:T(8,128)}, bf16[1024,384]{1,0:T(8,128)(2,1)}, bf16[1024,768]{1,0:T(8,128)(2,1)}, bf16[102...) custom-call(s32[8,1024]{1,0:T(8,128)} %add_add_fusion.refs_0_, ...), custom_call_target="tpu_custom_call" | custom-call | tf_op jit(solution)/shard_map/pallas_call | solution.py:42
  111.5 0.0 collective-permute-done
  111.5 0.6 fusion.3
  112.1 56.0 %shard_map.374 = (f32[1024,768]{1,0:T(8,128)}, bf16[1024,768]{1,0:T(8,128)(2,1)}, bf16[1024,1152]{1,0:T(8,128)(2,1)}, bf16[1024,384]{1,0:T(8,128)(2,1)}, f32[6,1...) custom-call(bf16[1024,768]{1,0:T(8,128)(2,1)} %get-tuple-element.78., ...), custom_call_target="tpu_custom_call" | custom-call | tf_op jit(solution)/shard_map/pallas_call | solution.py:42
  168.1 0.6 slice.92.refs_9_
  168.7 21.8 %shard_map.375 = (f32[1024,768]{1,0:T(8,128)}, f32[1024,1]{1,0:T(8,128)}, bf16[1024,768]{1,0:T(8,128)(2,1)}, bf16[1024,1536]{1,0:T(8,128)(2,1)}, bf16[1024,1536]...) custom-call(f32[1024,768]{1,0:T(8,128)} %get-tuple-element.83.refs_0_, ...), custom_call_target="tpu_custom_call" | custom-call | tf_op jit(solution)/shard_map/pallas_call | solution.py:42
  190.5 46.7 %shard_map.376 = (bf16[1024,768]{1,0:T(8,128)(2,1)}, f32[1024,768]{1,0:T(8,128)}, bf16[1024,768]{1,0:T(8,128)(2,1)}, bf16[4,2,2,48,768]{4,3,2,1,0:T(8,128)(2,1)}...) custom-call(f32[1024,768]{1,0:T(8,128)} %get-tuple-element.90.refs_0, ...), custom_call_target="tpu_custom_call" | custom-call | tf_op jit(solution)/shard_map/pallas_call | solution.py:42
  237.3 77.1 %shard_map.377 = (bf16[4,2,2,48,768]{4,3,2,1,0:T(8,128)(2,1)}, bf16[4,2,2,48,768]{4,3,2,1,0:T(8,128)(2,1)}, f32[3,768]{1,0:T(4,128)}, f32[1,1152]{1,0:T(1,128)},...) custom-call(f32[1024,768]{1,0:T(8,128)} %get-tuple-element.101.refs_, ...), custom_call_target="tpu_custom_call" | custom-call | tf_op jit(solution)/shard_map/pallas_call | solution.py:42
  314.4 0.0 copy-start.5
  314.4 0.0 copy-start.6
  314.4 0.0 copy-start.3
  314.4 0.0 copy-start.4
  314.4 94.1 %shard_map.378 = (f32[1024,384]{1,0:T(8,128)}, f32[384,384]{1,0:T(8,128)}, f32[48,768]{1,0:T(8,128)}, f32[48,768]{1,0:T(8,128)}, f32[16,768]{1,0:T(8,128)}, /*index=5*/f32[2,768]{1,0:T(2,128)}, f32[4,128]{1,0:T(4,128)}) custom-call(s32[8,1024]{1,0:T(8,128)} %add_add_fusion.refs_0_, bf16[384,1536]{1,0:T(8,128)(2,1)} %get-tuple-element.98.refs_1_, ...), custom_call_target="tpu_custom_call" | custom-call | tf_op jit(solution)/shard_map/pallas_call | solution.py:42
  408.5 0.0 copy-start
  408.5 1.7 fusion
  410.2 1.6 slice_bitcast_fusion
  411.8 1.9 slice_reduce_fusion
  413.7 0.6 dynamic-slice_reduce_fusion
  414.3 0.6 dynamic-slice_reduce_fusion.1
  414.9 0.6 dynamic-slice_reduce_fusion.2
  415.5 0.6 dynamic-slice_reduce_fusion.3
  416.1 1.3 reshape.73
  417.4 1.3 slice_reduce_fusion.6
  418.7 0.0 copy-done.5
  418.7 0.0 copy-done.6
  418.7 0.7 maximum_bitcast_fusion
  419.4 0.0 copy-done.3
  419.4 0.0 copy-done.4
  419.4 0.7 pad_maximum_fusion
  420.2 0.0 copy-done
  420.2 0.0 copy-start.1
  420.2 1.1 copy.48
  421.3 0.8 copy-done.1
  422.2 0.0 copy-start.2
  422.2 1.1 copy.49
  423.3 0.3 copy-done.2
  423.6 0.8 copy.50
  (2 shorter events, 0.0 us)
Async XLA Ops:
  0.7 15.7 %copy-start.7 = (bf16[768]{0:T(1024)(128)(2,1)S(1)}, bf16[768]{0:T(1024)(128)(2,1)}, u32[]{:S(2)}) copy-start(bf16[768]{0:T(1024)(128)(2,1)} %param.40) | copy-start | bytes 4612
  0.7 16.3 %copy-start.8 = (bf16[768]{0:T(1024)(128)(2,1)S(1)}, bf16[768]{0:T(1024)(128)(2,1)}, u32[]{:S(2)}) copy-start(bf16[768]{0:T(1024)(128)(2,1)} %param.41) | copy-start | bytes 4612
  0.7 16.9 %copy-start.9 = (bf16[768]{0:T(1024)(128)(2,1)S(1)}, bf16[768]{0:T(1024)(128)(2,1)}, u32[]{:S(2)}) copy-start(bf16[768]{0:T(1024)(128)(2,1)} %param.42) | copy-start | bytes 4612
  1.4 110.1 %collective-permute-start = (bf16[1,2304]{1,0:T(2,128)(2,1)S(1)}, bf16[1,2304]{1,0:T(2,128)(2,1)S(1)}, u32[]{:S(2)}, u32[]{:S(2)}) collective-permute-start(bf16[1,2304]{1,0:T(2,128)(2,1)S(1)} %broadcast_in_dim.57), channel_id=1, source_target_pairs={{0,0},{1,2},{2,1},{3,3},{4,4},{5,6},{6,5},{7,7},{8,8},{9,10},{10,9... | collective-permute-start | bytes 13832 | tf_op jit(solution)/shard_map/ppermute | solution.py:1003
  314.4 104.3 %copy-start.5 = (f32[48,768]{1,0:T(8,128)S(1)}, f32[48,768]{1,0:T(8,128)}, u32[]{:S(2)}) copy-start(f32[48,768]{1,0:T(8,128)} %get-tuple-element.132) | copy-start | bytes 442372
  314.4 104.3 %copy-start.6 = (f32[48,768]{1,0:T(8,128)S(1)}, f32[48,768]{1,0:T(8,128)}, u32[]{:S(2)}) copy-start(f32[48,768]{1,0:T(8,128)} %get-tuple-element.133) | copy-start | bytes 442372
  314.4 105.0 %copy-start.3 = (f32[48,768]{1,0:T(8,128)S(1)}, f32[48,768]{1,0:T(8,128)}, u32[]{:S(2)}) copy-start(f32[48,768]{1,0:T(8,128)} %get-tuple-element.129) | copy-start | bytes 442372
  314.4 105.0 %copy-start.4 = (f32[48,768]{1,0:T(8,128)S(1)}, f32[48,768]{1,0:T(8,128)}, u32[]{:S(2)}) copy-start(f32[48,768]{1,0:T(8,128)} %get-tuple-element.130) | copy-start | bytes 442372
  408.5 11.7 %copy-start = (bf16[1024,768]{1,0:T(8,128)(2,1)S(1)}, bf16[1024,768]{1,0:T(8,128)(2,1)}, u32[]{:S(2)}) copy-start(bf16[1024,768]{1,0:T(8,128)(2,1)} %get-tuple-element.97) | copy-start | bytes 4718596
  420.2 2.0 copy-start.1
  422.2 1.5 copy-start.2
